TPU v7x, 32 devices: a whole 2x2x4 slice. The times are simulated.
32 devices in a mesh: seq: 32 (over z, y, x, core).
Axes of the slice: x: 2, y: 2, z: 4, core: 2. Of those that a mesh axis runs over, the one named last changes fastest.
Arguments:
- tokens: bfloat16 [16384, 192], P('seq'), may hold values from -6 to 6
- out_grad: bfloat16 [16384, 192], P('seq'), may hold values from -6 to 6
- spread_weight: bfloat16 [384, 768], replicated, may hold values from -0.3125 to 0.3125
- merge_weight: bfloat16 [768, 384], replicated, may hold values from -0.21875 to 0.21875
- switch_bias: float32 [384], replicated, may hold values from -4 to 4
- gate_logit: float32 [384], replicated, may hold values from -1 to 3
Outputs:
- network_out: bfloat16 [16384, 192], P('seq')
- token_grad: bfloat16 [16384, 192], P('seq')
- spread_grad: float32 [384, 768], replicated
- merge_grad: float32 [768, 384], replicated
- bias_grad: float32 [384], replicated
- gate_grad: float32 [384], replicated
All inputs are finite; a program needn't handle non-finite values.
Results may differ from a plain program's by a relative error of at most 0.008.
Values may be sent and summed in bfloat16 or wider, within the bound.
A program may use at most 64 MiB of HBM per device.

v0:
```python
import math

import jax
import jax.numpy as jnp
from jax import lax
from jax.sharding import PartitionSpec as P

SECTIONS = 4


sqrt_half = 0.7071067811865476
inv_sqrt_two_pi = 0.3989422804014327


def swapped(value, axis, stride):
    mask = 2**stride
    pairs = [(source, source ^ mask) for source in range(lax.axis_size(axis))]
    return lax.ppermute(value, axis, pairs)


def gelu_exact(values):
    return 0.5 * values * (1.0 + lax.erf(values * sqrt_half))


def gelu_slope(values):
    return (
        0.5 * (1.0 + lax.erf(values * sqrt_half))
        + values * jnp.exp(-0.5 * values * values) * inv_sqrt_two_pi
    )


def normalize(pre_norm):
    centered = pre_norm - jnp.mean(pre_norm, -1, keepdims=True)
    inv_scale = lax.rsqrt(jnp.mean(centered * centered, -1, keepdims=True) + 1e-05)
    return (centered * inv_scale, inv_scale)


def switch_forward(paired, spread_weight, merge_weight, switch_bias, gate_logit):
    pre_norm = jnp.dot(paired, spread_weight, preferred_element_type=jnp.float32)
    normed, inv_scale = normalize(pre_norm)
    hidden = gelu_exact(normed).astype(jnp.bfloat16)
    branch = jnp.dot(hidden, merge_weight, preferred_element_type=jnp.float32) + switch_bias
    return (jax.nn.sigmoid(gate_logit) * paired.astype(jnp.float32) + 0.25 * branch).astype(
        jnp.bfloat16
    )


def switch_backward(paired, grad_pairs, spread_weight, merge_weight, gate_logit):
    pre_norm = jnp.dot(paired, spread_weight, preferred_element_type=jnp.float32)
    normed, inv_scale = normalize(pre_norm)
    hidden = gelu_exact(normed).astype(jnp.bfloat16)
    grad_rows = grad_pairs.astype(jnp.float32)
    branch_grad = (0.25 * grad_rows).astype(jnp.bfloat16)
    hidden_grad = lax.dot_general(
        branch_grad, merge_weight, (((1,), (1,)), ((), ())), preferred_element_type=jnp.float32
    )
    normed_grad = hidden_grad * gelu_slope(normed)
    pre_grad = inv_scale * (
        normed_grad
        - jnp.mean(normed_grad, -1, keepdims=True)
        - normed * jnp.mean(normed_grad * normed, -1, keepdims=True)
    )
    pre_grad = pre_grad.astype(jnp.bfloat16)
    back_rows = lax.dot_general(
        pre_grad, spread_weight, (((1,), (1,)), ((), ())), preferred_element_type=jnp.float32
    )
    paired_grad = (jax.nn.sigmoid(gate_logit) * grad_rows + back_rows).astype(jnp.bfloat16)
    masked_grad, masked_branch, masked_pre = (grad_rows, branch_grad, pre_grad)
    gate_term = jnp.sum(masked_grad * paired.astype(jnp.float32), 0)
    bias_term = 0.25 * jnp.sum(masked_grad, 0)
    merge_term = lax.dot_general(
        hidden, masked_branch, (((0,), (0,)), ((), ())), preferred_element_type=jnp.float32
    )
    spread_term = lax.dot_general(
        paired, masked_pre, (((0,), (0,)), ((), ())), preferred_element_type=jnp.float32
    )
    return (paired_grad, (spread_term, merge_term, bias_term, gate_term))


def on_device(tokens, out_grad, spread_weight, merge_weight, switch_bias, gate_logit):
    row_count, unit_count = tokens.shape
    device_bits = lax.axis_size("seq").bit_length() - 1
    grad_scale = 1.0 / math.sqrt(lax.axis_size("seq") * row_count)
    position = lax.axis_index("seq")
    group_size = 2**SECTIONS
    sub_rows = row_count // group_size

    def upper_side(bit_num):
        return position // 2**bit_num % 2 == 1

    def regroup(rows):
        blocks = rows.reshape(group_size, sub_rows, unit_count)
        for bit_pos in range(SECTIONS):
            device_bit = device_bits - SECTIONS + bit_pos
            is_upper = upper_side(device_bit)
            viewed = blocks.reshape(
                group_size // 2 ** (bit_pos + 1), 2, 2**bit_pos, sub_rows, unit_count
            )
            low_slot = viewed[:, 0]
            high_slot = viewed[:, 1]
            kept_blocks = jnp.where(is_upper, high_slot, low_slot)
            outgoing = jnp.where(is_upper, low_slot, high_slot).reshape(-1, 2 * unit_count)
            incoming = swapped(outgoing, "seq", device_bit).reshape(kept_blocks.shape)
            new_low = jnp.where(is_upper, incoming, kept_blocks)
            new_high = jnp.where(is_upper, kept_blocks, incoming)
            blocks = jnp.stack([new_low, new_high], 1).reshape(group_size, sub_rows, unit_count)
        return blocks.reshape(row_count, unit_count)

    def local_pairs(rows, section_num):
        viewed = rows.reshape(2**section_num, 2, -1, unit_count)
        return jnp.concatenate([viewed[:, 0], viewed[:, 1]], -1).reshape(-1, 2 * unit_count)

    def local_split(result, section_num):
        viewed = result.reshape(2**section_num, -1, 2 * unit_count)
        return jnp.stack([viewed[..., :unit_count], viewed[..., unit_count:]], 1).reshape(
            row_count, unit_count
        )

    spread_total = jnp.zeros(spread_weight.shape, jnp.float32)
    merge_total = jnp.zeros(merge_weight.shape, jnp.float32)
    bias_total = jnp.zeros(switch_bias.shape, jnp.float32)
    gate_total = jnp.zeros(gate_logit.shape, jnp.float32)
    saved = []
    current = regroup(tokens)
    for section_num in range(SECTIONS):
        paired = local_pairs(current, section_num)
        saved.append(paired)
        current = local_split(
            switch_forward(paired, spread_weight, merge_weight, switch_bias, gate_logit),
            section_num,
        )
    network_out = regroup(current)
    grad_rows = regroup(out_grad)
    for section_num in reversed(range(SECTIONS)):
        grad_pairs = local_pairs(grad_rows, section_num)
        paired_grad, term_list = switch_backward(
            saved[section_num], grad_pairs, spread_weight, merge_weight, gate_logit
        )
        spread_total = spread_total + term_list[0]
        merge_total = merge_total + term_list[1]
        bias_total = bias_total + term_list[2]
        gate_total = gate_total + term_list[3]
        grad_rows = local_split(paired_grad, section_num)
    grad_rows = regroup(grad_rows)
    spread_sum, merge_sum, bias_sum, gate_sum = lax.psum(
        (spread_total, merge_total, bias_total, gate_total), "seq"
    )
    gate_open = jax.nn.sigmoid(gate_logit)
    return (
        network_out,
        grad_rows,
        spread_sum * grad_scale,
        merge_sum * grad_scale,
        bias_sum * grad_scale,
        gate_sum * gate_open * (1.0 - gate_open) * grad_scale,
    )


def solution(mesh):
    placed = (P("seq", None), P("seq", None), P(), P(), P(), P())
    return jax.shard_map(
        on_device,
        mesh=mesh,
        in_specs=placed,
        out_specs=(P("seq", None), P("seq", None), P(), P(), P(), P()),
        check_vma=False,
    )
```

profile of v0, /device:TPU:0, one launch (start us, length us, event | category | flops | bytes accessed | tf_op | source)
XLA Modules:
  0.0 259.8 jit_solution(574415142809660923)
XLA Ops:
  7.3 1.1 copy.31
  8.6 3.0 %collective-permute-start.8 = (bf16[128,384]{1,0:T(8,128)(2,1)S(1)}, bf16[128,384]{1,0:T(8,128)(2,1)S(1)}, u32[]{:S(2)}, u32[]{:S(2)}) collective-permute-start(bf16[128,384]{1,0:T(8,128)(2,1)S(1)} %select_n.593), channel_id=1, source_target_pairs={{0,2},{1,3},{2,0},{3,1},{4,6},{5,7},{6,4},{7,5},{8,10},{9,11},{10,... | collective-permute-start | bytes 294920 | tf_op jit(solution)/shard_map/ppermute | solution.py:18
  12.1 2.6 %collective-permute-done.8 = bf16[128,384]{1,0:T(8,128)(2,1)S(1)} collective-permute-done((bf16[128,384]{1,0:T(8,128)(2,1)S(1)}, bf16[128,384]{1,0:T(8,128)(2,1)S(1)}, u32[]{:S(2)}, u32[]{:S(2)}) %collective-permute-start.8) | collective-permute-done | bytes 98336 | tf_op jit(solution)/shard_map/ppermute | solution.py:18
  15.1 2.3 collective-permute-start.9
  17.7 1.0 collective-permute-start.1
  18.8 2.2 collective-permute-done.9
  21.4 1.9 collective-permute-start.10
  23.7 0.8 collective-permute-start.2
  24.5 1.8 collective-permute-done.10
  26.6 3.6 %collective-permute-start.11 = (bf16[128,384]{1,0:T(8,128)(2,1)S(1)}, bf16[128,384]{1,0:T(8,128)(2,1)S(1)}, u32[]{:S(2)}, u32[]{:S(2)}) collective-permute-start(bf16[128,384]{1,0:T(8,128)(2,1)S(1)} %select_n.608), channel_id=1, source_target_pairs={{0,16},{1,17},{2,18},{3,19},{4,20},{5,21},{6,22},{7,23},{8,24},{9,... | collective-permute-start | bytes 294920 | tf_op jit(solution)/shard_map/ppermute | solution.py:18
  30.7 1.2 collective-permute-start.3
  31.9 1.0 collective-permute-done.11
  33.2 3.1 %collective-permute-done.3 = bf16[128,384]{1,0:T(8,128)(2,1)S(1)} collective-permute-done((bf16[128,384]{1,0:T(8,128)(2,1)S(1)}, bf16[128,384]{1,0:T(8,128)(2,1)S(1)}, u32[]{:S(2)}, u32[]{:S(2)}) %collective-permute-start.3) | collective-permute-done | bytes 98336 | tf_op jit(solution)/shard_map/ppermute | solution.py:18
  36.4 0.5 fusion.82
  38.5 0.5 fusion.83
  39.5 0.4 fusion.9
  40.3 0.5 fusion.84
  42.1 0.5 fusion.85
  42.8 1.2 fusion.75
  44.1 0.4 multiply_convert_fusion.3
  44.5 0.4 fusion.12
  45.1 1.0 fusion.74
  46.8 0.4 fusion.13
  47.6 1.0 fusion.73
  49.1 0.4 fusion.14
  50.2 0.4 fusion.67
  50.6 2.1 fusion.72
  52.7 1.5 fusion.49
  54.2 1.0 fusion.11
  55.2 0.6 add_multiply_fusion
  55.8 40.1 %all-reduce = (f32[384]{0:T(512)}, f32[384]{0:T(512)}) all-reduce(f32[384]{0:T(512)} %add_multiply_fusion, f32[384]{0:T(512)S(1)} %add_add_fusion), channel_id=1, replica_groups=mesh['seq'=32] {'seq'}, use_global_device_ids=true, to_apply=%region_22.23 | all-reduce | flops 768 | bytes 6144 | tf_op jit(solution)/shard_map/psum | solution.py:145
  95.9 1.3 multiply_multiply_fusion.4
  97.2 2.0 convolution_add_fusion.2
  99.2 0.5 convolution_add_fusion.1
  99.7 0.5 copy-done.13
  100.2 1.5 convolution_add_fusion
  101.7 0.4 convolution_add_fusion.5
  102.2 0.4 copy-done.5
  102.8 0.4 convolution_add_fusion.4
  103.5 0.4 copy-done.32
  104.2 0.4 fusion.17
  104.6 0.5 copy-done.3
  105.1 1.4 convolution_add_fusion.3
  106.9 2.3 collective-permute-start.12
  109.4 0.6 broadcast_multiply_fusion.2
  110.2 0.6 collective-permute-start.4
  110.8 1.3 collective-permute-done.12
  112.5 2.5 collective-permute-start.13
  115.4 1.5 collective-permute-start.5
  116.9 1.8 collective-permute-done.13
  119.1 1.7 collective-permute-start.14
  120.8 0.5 collective-permute-done.5
  121.7 1.6 collective-permute-start.6
  123.3 3.7 %collective-permute-done.14 = bf16[128,384]{1,0:T(8,128)(2,1)S(1)} collective-permute-done((bf16[128,384]{1,0:T(8,128)(2,1)S(1)}, bf16[128,384]{1,0:T(8,128)(2,1)S(1)}, u32[]{:S(2)}, u32[]{:S(2)}) %collective-permute-start.14) | collective-permute-done | bytes 98336 | tf_op jit(solution)/shard_map/ppermute | solution.py:18
  127.3 1.5 collective-permute-start.15
  128.8 1.3 collective-permute-done.6
  130.5 2.3 collective-permute-start.7
  132.8 4.3 %collective-permute-done.15 = bf16[128,384]{1,0:T(8,128)(2,1)S(1)} collective-permute-done((bf16[128,384]{1,0:T(8,128)(2,1)S(1)}, bf16[128,384]{1,0:T(8,128)(2,1)S(1)}, u32[]{:S(2)}, u32[]{:S(2)}) %collective-permute-start.15) | collective-permute-done | bytes 98336 | tf_op jit(solution)/shard_map/ppermute | solution.py:18
  137.4 0.8 copy.42
  138.2 1.9 collective-permute-done.7
  140.3 0.8 copy.41
  141.1 108.3 %all-reduce.4.cloned.1.call-done = (f32[384,768]{1,0:T(8,128)}, f32[768,384]{1,0:T(8,128)}) async-done(((f32[384,768]{1,0:T(8,128)}, f32[768,384]{1,0:T(8,128)}), (f32[384,768]{1,0:T(8,128)}, f32[768,384]{1,0:T(8,128)})) %all-reduce.4.cloned.1.call-update) | async-done | bytes 2359312 | tf_op jit(solution)/shard_map/psum | solution.py:145
  249.4 2.5 broadcast_multiply_fusion
  251.9 1.1 broadcast_multiply_fusion.1
  (228 shorter events, 13.0 us)
Async XLA Ops:
  7.2 30.3 %copy-start = (bf16[768,384]{1,0:T(8,128)(2,1)S(1)}, bf16[768,384]{1,0:T(8,128)(2,1)}, u32[]{:S(2)}) copy-start(bf16[768,384]{1,0:T(8,128)(2,1)} %param.9) | copy-start | bytes 1769476
  7.2 4.4 %copy-start.34 = (bf16[512,192]{0,1:T(8,128)(2,1)S(1)}, bf16[512,192]{0,1:T(8,128)(2,1)}, u32[]{:S(2)}) copy-start(bf16[512,192]{0,1:T(8,128)(2,1)} %param.6) | copy-start | bytes 589828
  7.2 4.8 %copy-start.35 = (f32[384]{0:T(512)S(1)}, f32[384]{0:T(512)}, u32[]{:S(2)}) copy-start(f32[384]{0:T(512)} %param.11) | copy-start | bytes 4612
  7.2 242.2 %all-reduce.4.cloned.1.call-start = ((), (), s32[]{:S(2)}) async-start(), calls=%async_computation | async-start | bytes 4718592 | tf_op jit(solution)/shard_map/psum | solution.py:145
  8.6 6.1 %collective-permute-start.8 = (bf16[128,384]{1,0:T(8,128)(2,1)S(1)}, bf16[128,384]{1,0:T(8,128)(2,1)S(1)}, u32[]{:S(2)}, u32[]{:S(2)}) collective-permute-start(bf16[128,384]{1,0:T(8,128)(2,1)S(1)} %select_n.593), channel_id=1, source_target_pairs={{0,2},{1,3},{2,0},{3,1},{4,6},{5,7},{6,4},{7,5},{8,10},{9,11},{10,... | collective-permute-start | bytes 294920 | tf_op jit(solution)/shard_map/ppermute | solution.py:18
  11.9 5.5 %collective-permute-start = (bf16[128,384]{1,0:T(8,128)(2,1)S(1)}, bf16[128,384]{1,0:T(8,128)(2,1)S(1)}, u32[]{:S(2)}, u32[]{:S(2)}) collective-permute-start(bf16[128,384]{1,0:T(8,128)(2,1)S(1)} %select_n.553), channel_id=1, source_target_pairs={{0,2},{1,3},{2,0},{3,1},{4,6},{5,7},{6,4},{7,5},{8,10},{9,11},{10,... | collective-permute-start | bytes 294920 | tf_op jit(solution)/shard_map/ppermute | solution.py:18
  12.0 42.2 %copy-start.36 = (f32[384]{0:T(512)}, f32[384]{0:T(512)S(1)}, u32[]{:S(2)}) copy-start(f32[384]{0:T(512)S(1)} %add_divide_fusion) | copy-start | bytes 4612
  15.1 5.9 %collective-permute-start.9 = (bf16[128,384]{1,0:T(8,128)(2,1)S(1)}, bf16[128,384]{1,0:T(8,128)(2,1)S(1)}, u32[]{:S(2)}, u32[]{:S(2)}) collective-permute-start(bf16[128,384]{1,0:T(8,128)(2,1)S(1)} %select_n.598), channel_id=1, source_target_pairs={{0,4},{1,5},{2,6},{3,7},{4,0},{5,1},{6,2},{7,3},{8,12},{9,13},{10,... | collective-permute-start | bytes 294920 | tf_op jit(solution)/shard_map/ppermute | solution.py:18
  17.7 5.5 %collective-permute-start.1 = (bf16[128,384]{1,0:T(8,128)(2,1)S(1)}, bf16[128,384]{1,0:T(8,128)(2,1)S(1)}, u32[]{:S(2)}, u32[]{:S(2)}) collective-permute-start(bf16[128,384]{1,0:T(8,128)(2,1)S(1)} %select_n.558), channel_id=1, source_target_pairs={{0,4},{1,5},{2,6},{3,7},{4,0},{5,1},{6,2},{7,3},{8,12},{9,13},{10,... | collective-permute-start | bytes 294920 | tf_op jit(solution)/shard_map/ppermute | solution.py:18
  21.4 4.9 %collective-permute-start.10 = (bf16[128,384]{1,0:T(8,128)(2,1)S(1)}, bf16[128,384]{1,0:T(8,128)(2,1)S(1)}, u32[]{:S(2)}, u32[]{:S(2)}) collective-permute-start(bf16[128,384]{1,0:T(8,128)(2,1)S(1)} %select_n.603), channel_id=1, source_target_pairs={{0,8},{1,9},{2,10},{3,11},{4,12},{5,13},{6,14},{7,15},{8,0},{9,1},... | collective-permute-start | bytes 294920 | tf_op jit(solution)/shard_map/ppermute | solution.py:18
  23.7 6.6 %collective-permute-start.2 = (bf16[128,384]{1,0:T(8,128)(2,1)S(1)}, bf16[128,384]{1,0:T(8,128)(2,1)S(1)}, u32[]{:S(2)}, u32[]{:S(2)}) collective-permute-start(bf16[128,384]{1,0:T(8,128)(2,1)S(1)} %select_n.563), channel_id=1, source_target_pairs={{0,8},{1,9},{2,10},{3,11},{4,12},{5,13},{6,14},{7,15},{8,0},{9,1},... | collective-permute-start | bytes 294920 | tf_op jit(solution)/shard_map/ppermute | solution.py:18
  26.6 6.3 %collective-permute-start.11 = (bf16[128,384]{1,0:T(8,128)(2,1)S(1)}, bf16[128,384]{1,0:T(8,128)(2,1)S(1)}, u32[]{:S(2)}, u32[]{:S(2)}) collective-permute-start(bf16[128,384]{1,0:T(8,128)(2,1)S(1)} %select_n.608), channel_id=1, source_target_pairs={{0,16},{1,17},{2,18},{3,19},{4,20},{5,21},{6,22},{7,23},{8,24},{9,... | collective-permute-start | bytes 294920 | tf_op jit(solution)/shard_map/ppermute | solution.py:18
  30.7 5.6 %collective-permute-start.3 = (bf16[128,384]{1,0:T(8,128)(2,1)S(1)}, bf16[128,384]{1,0:T(8,128)(2,1)S(1)}, u32[]{:S(2)}, u32[]{:S(2)}) collective-permute-start(bf16[128,384]{1,0:T(8,128)(2,1)S(1)} %select_n.568), channel_id=1, source_target_pairs={{0,16},{1,17},{2,18},{3,19},{4,20},{5,21},{6,22},{7,23},{8,24},{9,... | collective-permute-start | bytes 294920 | tf_op jit(solution)/shard_map/ppermute | solution.py:18
  33.0 3.4 %copy-start.1 = (bf16[384,768]{1,0:T(8,128)(2,1)S(1)}, bf16[384,768]{1,0:T(8,128)(2,1)}, u32[]{:S(2)}) copy-start(bf16[384,768]{1,0:T(8,128)(2,1)} %param.8) | copy-start | bytes 1769476
  33.1 13.1 %copy-start.21 = (bf16[8,1,32,192]{3,2,1,0:T(8,128)(2,1)}, bf16[8,1,32,192]{3,2,1,0:T(8,128)(2,1)S(1)}, u32[]{:S(2)}) copy-start(bf16[8,1,32,192]{3,2,1,0:T(8,128)(2,1)S(1)} %get-tuple-element.72) | copy-start | bytes 294916
  33.2 13.1 %copy-start.23 = (bf16[8,1,32,192]{3,2,1,0:T(8,128)(2,1)}, bf16[8,1,32,192]{3,2,1,0:T(8,128)(2,1)S(1)}, u32[]{:S(2)}) copy-start(bf16[8,1,32,192]{3,2,1,0:T(8,128)(2,1)S(1)} %get-tuple-element.73) | copy-start | bytes 294916
  36.4 13.5 %copy-start.2 = (bf16[1,1,8,32,192]{4,3,2,1,0:T(8,128)(2,1)}, bf16[1,1,8,32,192]{4,3,2,1,0:T(8,128)(2,1)S(1)}, u32[]{:S(2)}) copy-start(bf16[1,1,8,32,192]{4,3,2,1,0:T(8,128)(2,1)S(1)} %get-tuple-element.57) | copy-start | bytes 294916
  36.9 0.7 copy-start.41
  37.6 0.8 copy-start.12
  38.4 10.2 %copy-start.4 = (bf16[2,1,128,192]{3,2,1,0:T(8,128)(2,1)}, bf16[2,1,128,192]{3,2,1,0:T(8,128)(2,1)S(1)}, u32[]{:S(2)}) copy-start(bf16[2,1,128,192]{3,2,1,0:T(8,128)(2,1)S(1)} %get-tuple-element.82) | copy-start | bytes 294916
  38.5 10.2 %copy-start.6 = (bf16[2,1,128,192]{3,2,1,0:T(8,128)(2,1)}, bf16[2,1,128,192]{3,2,1,0:T(8,128)(2,1)S(1)}, u32[]{:S(2)}) copy-start(bf16[2,1,128,192]{3,2,1,0:T(8,128)(2,1)S(1)} %get-tuple-element.83) | copy-start | bytes 294916
  39.5 0.7 copy-start.14
  40.3 5.8 %copy-start.8 = (bf16[4,1,64,192]{3,2,1,0:T(8,128)(2,1)}, bf16[4,1,64,192]{3,2,1,0:T(8,128)(2,1)S(1)}, u32[]{:S(2)}) copy-start(bf16[4,1,64,192]{3,2,1,0:T(8,128)(2,1)S(1)} %get-tuple-element.80) | copy-start | bytes 294916
  40.3 5.8 %copy-start.10 = (bf16[4,1,64,192]{3,2,1,0:T(8,128)(2,1)}, bf16[4,1,64,192]{3,2,1,0:T(8,128)(2,1)S(1)}, u32[]{:S(2)}) copy-start(bf16[4,1,64,192]{3,2,1,0:T(8,128)(2,1)S(1)} %get-tuple-element.81) | copy-start | bytes 294916
  41.3 0.7 copy-start.16
  45.0 1.7 copy-start.26
  45.1 1.7 copy-start.27
  46.8 0.7 copy-start.17
  47.5 1.5 copy-start.28
  47.5 1.5 copy-start.30
  49.1 0.7 copy-start.19
  50.6 2.1 copy-start.22
  50.6 2.1 copy-start.24
  97.2 2.0 copy-start.15
  97.2 2.0 copy-start.29
  97.2 2.0 copy-start.31
  99.2 1.0 copy-start.13
  100.2 1.5 copy-start.9
  100.2 1.5 copy-start.11
  100.2 1.5 copy-start.18
  101.7 0.9 copy-start.5
  101.7 1.0 copy-start.7
  101.7 1.1 copy-start.20
  102.8 0.7 copy-start.40
  102.8 0.7 copy-start.39
  102.8 1.1 copy-start.32
  103.3 0.9 copy-start.37
  104.2 0.9 copy-start.3
  106.6 2.7 %copy-start.33 = (bf16[256,384]{1,0:T(8,128)(2,1)S(1)}, bf16[256,384]{1,0:T(8,128)(2,1)}, u32[]{:S(2)}) copy-start(bf16[256,384]{1,0:T(8,128)(2,1)} %fusion.11) | copy-start | bytes 589828
  106.7 2.8 %copy-start.38 = (f32[384]{0:T(512)S(1)}, f32[384]{0:T(512)}, u32[]{:S(2)}) copy-start(f32[384]{0:T(512)} %get-tuple-element.26) | copy-start | bytes 4612
  106.9 5.2 %collective-permute-start.12 = (bf16[128,384]{1,0:T(8,128)(2,1)S(1)}, bf16[128,384]{1,0:T(8,128)(2,1)S(1)}, u32[]{:S(2)}, u32[]{:S(2)}) collective-permute-start(bf16[128,384]{1,0:T(8,128)(2,1)S(1)} %select_n.613), channel_id=1, source_target_pairs={{0,2},{1,3},{2,0},{3,1},{4,6},{5,7},{6,4},{7,5},{8,10},{9,11},{10,... | collective-permute-start | bytes 294920 | tf_op jit(solution)/shard_map/ppermute | solution.py:18
  110.2 4.9 %collective-permute-start.4 = (bf16[128,384]{1,0:T(8,128)(2,1)S(1)}, bf16[128,384]{1,0:T(8,128)(2,1)S(1)}, u32[]{:S(2)}, u32[]{:S(2)}) collective-permute-start(bf16[128,384]{1,0:T(8,128)(2,1)S(1)} %select_n.573), channel_id=1, source_target_pairs={{0,2},{1,3},{2,0},{3,1},{4,6},{5,7},{6,4},{7,5},{8,10},{9,11},{10,... | collective-permute-start | bytes 294920 | tf_op jit(solution)/shard_map/ppermute | solution.py:18
  112.5 6.2 %collective-permute-start.13 = (bf16[128,384]{1,0:T(8,128)(2,1)S(1)}, bf16[128,384]{1,0:T(8,128)(2,1)S(1)}, u32[]{:S(2)}, u32[]{:S(2)}) collective-permute-start(bf16[128,384]{1,0:T(8,128)(2,1)S(1)} %select_n.618), channel_id=1, source_target_pairs={{0,4},{1,5},{2,6},{3,7},{4,0},{5,1},{6,2},{7,3},{8,12},{9,13},{10,... | collective-permute-start | bytes 294920 | tf_op jit(solution)/shard_map/ppermute | solution.py:18
  115.4 5.9 %collective-permute-start.5 = (bf16[128,384]{1,0:T(8,128)(2,1)S(1)}, bf16[128,384]{1,0:T(8,128)(2,1)S(1)}, u32[]{:S(2)}, u32[]{:S(2)}) collective-permute-start(bf16[128,384]{1,0:T(8,128)(2,1)S(1)} %select_n.578), channel_id=1, source_target_pairs={{0,4},{1,5},{2,6},{3,7},{4,0},{5,1},{6,2},{7,3},{8,12},{9,13},{10,... | collective-permute-start | bytes 294920 | tf_op jit(solution)/shard_map/ppermute | solution.py:18
  119.1 7.9 %collective-permute-start.14 = (bf16[128,384]{1,0:T(8,128)(2,1)S(1)}, bf16[128,384]{1,0:T(8,128)(2,1)S(1)}, u32[]{:S(2)}, u32[]{:S(2)}) collective-permute-start(bf16[128,384]{1,0:T(8,128)(2,1)S(1)} %select_n.623), channel_id=1, source_target_pairs={{0,8},{1,9},{2,10},{3,11},{4,12},{5,13},{6,14},{7,15},{8,0},{9,1},... | collective-permute-start | bytes 294920 | tf_op jit(solution)/shard_map/ppermute | solution.py:18
  121.7 8.4 %collective-permute-start.6 = (bf16[128,384]{1,0:T(8,128)(2,1)S(1)}, bf16[128,384]{1,0:T(8,128)(2,1)S(1)}, u32[]{:S(2)}, u32[]{:S(2)}) collective-permute-start(bf16[128,384]{1,0:T(8,128)(2,1)S(1)} %select_n.583), channel_id=1, source_target_pairs={{0,8},{1,9},{2,10},{3,11},{4,12},{5,13},{6,14},{7,15},{8,0},{9,1},... | collective-permute-start | bytes 294920 | tf_op jit(solution)/shard_map/ppermute | solution.py:18
  127.3 9.8 %collective-permute-start.15 = (bf16[128,384]{1,0:T(8,128)(2,1)S(1)}, bf16[128,384]{1,0:T(8,128)(2,1)S(1)}, u32[]{:S(2)}, u32[]{:S(2)}) collective-permute-start(bf16[128,384]{1,0:T(8,128)(2,1)S(1)} %select_n.628), channel_id=1, source_target_pairs={{0,16},{1,17},{2,18},{3,19},{4,20},{5,21},{6,22},{7,23},{8,24},{9,... | collective-permute-start | bytes 294920 | tf_op jit(solution)/shard_map/ppermute | solution.py:18
  130.5 9.6 %collective-permute-start.7 = (bf16[128,384]{1,0:T(8,128)(2,1)S(1)}, bf16[128,384]{1,0:T(8,128)(2,1)S(1)}, u32[]{:S(2)}, u32[]{:S(2)}) collective-permute-start(bf16[128,384]{1,0:T(8,128)(2,1)S(1)} %select_n.588), channel_id=1, source_target_pairs={{0,16},{1,17},{2,18},{3,19},{4,20},{5,21},{6,22},{7,23},{8,24},{9,... | collective-permute-start | bytes 294920 | tf_op jit(solution)/shard_map/ppermute | solution.py:18
  249.4 2.5 copy-start.25
Sparse Core Ops, SparseCore 0:
  110.9 138.4 all-reduce.3
where the time goes:
time: 260 us
  waiting for transfers between devices  134 us (52%)
  blocking collectives  40.1 us (15%)
  starting transfers between devices  28 us (11%)
  matrix products  19.2 us (7%)
  between operations  15.5 us (6%)
  local copies, waits for them, and re-layouts  11.6 us (4%)
  other arithmetic  11.5 us (4%)
    psum x1, waiting for transfers between devices, on_device(): lax.psum((spread_total, merge_total, bias_total, gate_total), 'seq')  108 us
    psum x1, blocking collectives, on_device(): lax.psum((spread_total, merge_total, bias_total, gate_total), 'seq')  40.1 us
    ppermute x16, starting transfers between devices, swapped(): return lax.ppermute(value, axis, pairs)  28 us
    ppermute x16, waiting for transfers between devices, swapped(): return lax.ppermute(value, axis, pairs)  25.6 us
    unnamed x88, local copies, waits for them, and re-layouts  6.56 us
    dot_general x4, matrix products, switch_backward(): lax.dot_general(hidden, masked_branch, (((0,), (0,)), ((), ())), preferre...  5.39 us
    dot_general x4, matrix products, switch_backward(): lax.dot_general(branch_grad, merge_weight, (((1,), (1,)), ((), ())), pref...  5.35 us
  transfers between devices with their start and end apart: 17, of which 13 were waited for; matrix products, arithmetic and copies ran while one was open for 3% of the time, Pallas kernels for 0%

commit v1 on v0

v1 whole, which is shorter than its diff:
```python
import functools
import math

import jax
import jax.numpy as jnp
from jax import lax
from jax.experimental import pallas as pl
from jax.experimental.pallas import tpu as pltpu
from jax.sharding import PartitionSpec as P

SECTIONS = 4
GROUP = 2**SECTIONS
SIDE = 4
LANES = 128
MESH = pl.DeviceIdType.MESH
F32 = jnp.float32
BF16 = jnp.bfloat16

sqrt_half = 0.7071067811865476
inv_sqrt_two_pi = 0.3989422804014327


def dot(a, b):
    return jnp.dot(a, b, preferred_element_type=F32)


def rounded_up(size):
    return -(-size // LANES) * LANES


def step_kernel(
    n,
    tok, og, sw, mw, bias, gate,
    net_o, tg_o, res, vec_o,
    sw_v, mw_v, bias_v, gate_v,
    xin, gin, xs, gs,
    state, wp, wt, mp, mt, rows_v,
    sides, wides, r_sides, r_wides,
    pre, normed, slope, inv,
    flat, flat_b, part, part_b, rv1, rv2, rvx, last,
    sums, v0, v1, v2, v3, rvm, rvv1, rvv2, rvvx,
    load_sem, a2a_sem, mate_sem, rs1_sem, rs2_sem, rsx_sem, ag1_sem, ag2_sem, fwd_sem,
    vm_sem, vv1_sem, vv2_sem, vvx_sem,
):
    rows, units = xin.shape
    sub = rows // GROUP
    half = rows // 2
    hidden_size = sw_v.shape[1]
    stride = n // GROUP
    others = n // (2 * GROUP)
    quarter = flat.shape[0] // SIDE
    piece = quarter // SIDE

    me = lax.axis_index("seq")
    top = me // stride
    low = me % stride
    core = me % 2
    mid = low // 2
    mate = me + 1 - 2 * core
    col = top % SIDE
    line = top // SIDE

    def dev(which):
        return which * stride + low

    def mid_dev(which):
        return top * stride + which * 2 + core

    def remote(src, dst, sems, target):
        return pltpu.make_async_remote_copy(
            src_ref=src, dst_ref=dst, send_sem=sems.at[0], recv_sem=sems.at[1],
            device_id=(target,), device_id_type=MESH,
        )

    loads = [
        pltpu.make_async_copy(tok.at[pl.ds(top * sub, sub)], xin.at[pl.ds(top * sub, sub)], load_sem.at[0]),
        pltpu.make_async_copy(og.at[pl.ds(top * sub, sub)], gin.at[pl.ds(top * sub, sub)], load_sem.at[1]),
        pltpu.make_async_copy(sw, sw_v, load_sem.at[2]),
        pltpu.make_async_copy(mw, mw_v, load_sem.at[3]),
        pltpu.make_async_copy(bias, bias_v, load_sem.at[4]),
        pltpu.make_async_copy(gate, gate_v, load_sem.at[5]),
    ]
    for load in loads:
        load.start()

    barrier = pltpu.get_barrier_semaphore()

    @pl.loop(1, GROUP)
    def _(j):
        pl.semaphore_signal(barrier, inc=1, device_id=(dev((top + j) % GROUP),), device_id_type=MESH)

    pl.semaphore_signal(barrier, inc=1, device_id=(mate,), device_id_type=MESH)
    for j in range(1, others):
        pl.semaphore_signal(
            barrier, inc=1, device_id=(mid_dev((mid + j) % others),), device_id_type=MESH
        )
    pl.semaphore_wait(barrier, GROUP + others - 1)

    def exchange(src, dst, number):
        def one(j):
            to = (top + j) % GROUP
            return remote(
                src.at[pl.ds(to * sub, sub)], dst.at[pl.ds(top * sub, sub)],
                a2a_sem.at[number, j], dev(to),
            )

        def start():
            @pl.loop(1, GROUP)
            def _(j):
                one(j).start()

        def received():
            @pl.loop(1, GROUP)
            def _(j):
                one(j).wait_recv()

        def sent():
            @pl.loop(1, GROUP)
            def _(j):
                one(j).wait_send()

        return start, received, sent

    tok_start, tok_received, tok_sent = exchange(tok, xin, 0)
    og_start, og_received, og_sent = exchange(og, gin, 1)
    net_start, net_received, net_sent = exchange(xs, net_o, 2)
    tg_start, tg_received, tg_sent = exchange(gs, tg_o, 3)
    tok_start()
    og_start()

    pad = wp.shape[1] - units
    loads[2].wait()
    loads[3].wait()
    turned = mw_v[...].T
    for h in range(2):
        wp[h, :units] = sw_v[h * units : (h + 1) * units]
        wp[h, units:] = jnp.zeros((pad, hidden_size), BF16)
        wt[h] = wp[h].T
        mt[h, :units] = turned[h * units : (h + 1) * units]
        mt[h, units:] = jnp.zeros((pad, hidden_size), BF16)
        mp[h] = mt[h].T
    loads[4].wait()
    loads[5].wait()
    rows_v[...] = jnp.zeros(rows_v.shape, F32)
    for h in range(2):
        rows_v[h : h + 1, :units] = jax.nn.sigmoid(gate_v[:, h * units : (h + 1) * units])
        rows_v[2 + h : 3 + h, :units] = bias_v[:, h * units : (h + 1) * units]
    sums[...] = jnp.zeros(sums.shape, F32)
    state[...] = jnp.zeros(state.shape, BF16)

    def spans(section):
        length = half >> section
        for k in range(2**section):
            for h in range(2):
                at = (2 * k + h) * length
                yield h, slice(k * length, (k + 1) * length), slice(at, at + length)

    chunk = 32
    loads[0].wait()
    tok_received()
    state[:, :units] = xin[...]
    for s in range(SECTIONS):
        for h, inner, outer in spans(s):
            sides[1, s, h, inner] = state[outer]
        pre[...] = dot(sides[1, s, 0], wp[0]) + dot(sides[1, s, 1], wp[1])

        @pl.loop(0, half // chunk)
        def _(i):
            at = pl.ds(pl.multiple_of(i * chunk, chunk), chunk)
            value = pre[at]
            centered = value - jnp.mean(value, -1, keepdims=True)
            scale = lax.rsqrt(jnp.mean(centered * centered, -1, keepdims=True) + 1e-05)
            value = centered * scale
            phi_sum = 0.5 * (1.0 + lax.erf(value * sqrt_half))
            wides[0, s, at] = (value * phi_sum).astype(BF16)
            normed[s, at] = value
            slope[s, at] = phi_sum + value * jnp.exp(-0.5 * value * value) * inv_sqrt_two_pi
            inv[s, at] = jnp.broadcast_to(scale, (chunk, LANES))

        outs = [
            (
                rows_v[h : h + 1] * sides[1, s, h].astype(F32)
                + 0.25 * (dot(wides[0, s], mp[h]) + rows_v[2 + h : 3 + h])
            ).astype(BF16)
            for h in range(2)
        ]
        for h, inner, outer in spans(s):
            if s < SECTIONS - 1:
                state[outer] = outs[h][inner]
            else:
                xs[outer] = outs[h][inner, :units]
    net_start()
    net_o[pl.ds(top * sub, sub)] = xs[pl.ds(top * sub, sub)]

    def gather_grads(side, wide, first):
        for h in range(2):
            term = dot(side[h].T[:units], wide[...])
            for c in range(hidden_size // LANES):
                at = slice((2 * c + h) * units, (2 * c + h + 1) * units)
                block = term[:, c * LANES : (c + 1) * LANES]
                flat[at] = block if first else flat[at] + block

    def mate_copies(s):
        return [
            remote(sides.at[1 - core, s], r_sides.at[s], mate_sem.at[0, s], mate),
            remote(wides.at[1 - core, s], r_wides.at[s], mate_sem.at[1, s], mate),
        ]

    vec_mate = remote(v0, rvm, vm_sem, mate)
    loads[1].wait()
    og_received()
    state[:, :units] = gin[...]
    for s in reversed(range(SECTIONS)):
        grads = [None, None]
        for h, inner, outer in spans(s):
            sides[0, s, h, inner] = (0.25 * state[outer].astype(F32)).astype(BF16)
        pre[...] = dot(sides[0, s, 0], mt[0]) + dot(sides[0, s, 1], mt[1])
        for h in range(2):
            value = 4.0 * sides[0, s, h].astype(F32)
            gated = value * sides[1, s, h].astype(F32)
            sums[h] += jnp.sum(value.reshape(-1, 8, value.shape[1]), 0)
            sums[2 + h] += jnp.sum(gated.reshape(-1, 8, value.shape[1]), 0)
        if s == 0:
            for r in range(4):
                v0[r : r + 1] = jnp.sum(sums[r], 0, keepdims=True)
            vec_mate.start()

        @pl.loop(0, half // chunk)
        def _(i):
            at = pl.ds(pl.multiple_of(i * chunk, chunk), chunk)
            value = normed[s, at]
            grad = pre[at] * slope[s, at]
            grad = (
                grad
                - jnp.mean(grad, -1, keepdims=True)
                - value * jnp.mean(grad * value, -1, keepdims=True)
            ) * inv[s, at][:, :1]
            wides[1, s, at] = grad.astype(BF16)

        for copy in mate_copies(s):
            copy.start()
        for h in range(2):
            back = dot(wides[1, s], wt[h])
            grads[h] = back
        for h, inner, outer in spans(s):
            value = (
                rows_v[h : h + 1] * (state[outer].astype(F32)) + grads[h][inner]
            ).astype(BF16)
            if s > 0:
                state[outer] = value
            else:
                gs[outer] = value[:, :units]
        if s == 0:
            tg_start()
            tg_o[pl.ds(top * sub, sub)] = gs[pl.ds(top * sub, sub)]
        gather_grads(sides.at[core, s], wides.at[core, s], s == SECTIONS - 1)
        if s < SECTIONS - 1:
            for copy in mate_copies(s + 1):
                copy.wait_recv()
            gather_grads(r_sides.at[s + 1], r_wides.at[s + 1], False)
    for copy in mate_copies(0):
        copy.wait_recv()
    gather_grads(r_sides.at[0], r_wides.at[0], False)
    flat_b[...] = flat[...].astype(BF16)

    def first_copies(j):
        to = (col + j) % SIDE
        target = dev(line * SIDE + to)
        return [
            remote(flat_b.at[pl.ds(to * quarter, quarter)], rv1.at[j - 1], rs1_sem.at[j], target),
            remote(v1, rvv1.at[j - 1], vv1_sem.at[j], target),
        ]

    def second_copies(j):
        to = (line + j) % SIDE
        target = dev(to * SIDE + col)
        return [
            remote(part_b.at[pl.ds(to * piece, piece)], rv2.at[j - 1], rs2_sem.at[j], target),
            remote(v2, rvv2.at[j - 1], vv2_sem.at[j], target),
        ]

    def other_copies(j):
        target = mid_dev((mid + j) % others)
        return [
            remote(last, rvx.at[j - 1], rsx_sem.at[j], target),
            remote(v3, rvvx.at[j - 1], vvx_sem.at[j], target),
        ]

    for j in range(1, SIDE):
        first_copies(j)[0].start()
    vec_mate.wait_recv()
    v1[...] = v0[...] + rvm[...]
    for j in range(1, SIDE):
        first_copies(j)[1].start()
    for j in range(1, SIDE):
        for copy in first_copies(j):
            copy.wait_recv()
    total = flat[pl.ds(pl.multiple_of(col * quarter, quarter), quarter)]
    for j in range(SIDE - 1):
        total = total + rv1[j].astype(F32)
    part[...] = total
    part_b[...] = total.astype(BF16)
    v2[...] = v1[...] + rvv1[0] + rvv1[1] + rvv1[2]
    for j in range(1, SIDE):
        for copy in second_copies(j):
            copy.start()
    for j in range(1, SIDE):
        for copy in second_copies(j):
            copy.wait_recv()
    total = part[pl.ds(pl.multiple_of(line * piece, piece), piece)]
    for j in range(SIDE - 1):
        total = total + rv2[j].astype(F32)
    vec = v2[...] + rvv2[0] + rvv2[1] + rvv2[2]
    if others > 1:
        last[...] = total.astype(BF16)
        v3[...] = vec
        for j in range(1, others):
            for copy in other_copies(j):
                copy.start()
        for j in range(1, others):
            for copy in other_copies(j):
                copy.wait_recv()
            total = total + rvx[j - 1].astype(F32)
            vec = vec + rvvx[j - 1]
    vec_o[...] = vec
    mine = pl.ds(pl.multiple_of(col * quarter + line * piece, piece), piece)
    res[core, mine] = total.astype(BF16)

    def line_copy(j):
        to = (line + j) % SIDE
        return remote(res.at[core, mine], res.at[core, mine], ag2_sem.at[j], dev(to * SIDE + col))

    whole = pl.ds(pl.multiple_of(col * quarter, quarter), quarter)

    def col_copy(j):
        to = (col + j) % SIDE
        return remote(res.at[core, whole], res.at[core, whole], ag1_sem.at[j], dev(line * SIDE + to))

    def mate_copy(j):
        at = (col + SIDE - j) % SIDE
        span = res.at[core, pl.ds(pl.multiple_of(at * quarter, quarter), quarter)]
        return remote(span, span, fwd_sem.at[j], mate)

    for j in range(1, SIDE):
        line_copy(j).start()
    for j in range(1, SIDE):
        line_copy(j).wait_recv()
    for j in range(1, SIDE):
        col_copy(j).start()
    mate_copy(0).start()
    for j in range(1, SIDE):
        col_copy(j).wait_recv()
        mate_copy(j).start()

    tok_sent()
    og_sent()
    net_sent()
    tg_sent()
    for s in range(SECTIONS):
        for copy in mate_copies(s):
            copy.wait_send()
    vec_mate.wait_send()
    for j in range(1, SIDE):
        for copy in first_copies(j) + second_copies(j) + [line_copy(j), col_copy(j)]:
            copy.wait_send()
    for j in range(1, others):
        for copy in other_copies(j):
            copy.wait_send()
    net_received()
    tg_received()
    for j in range(SIDE):
        mate_copy(j).wait()


def finish_kernel(scale, res, net, tg, vec, gate, net_o, tg_o, spread_o, merge_o, bias_o, gate_o):
    units = net.shape[1]
    tall, wide = spread_o.shape
    net_o[...] = net[...]
    tg_o[...] = tg[...]
    for c in range(wide // LANES):
        across = slice(c * LANES, (c + 1) * LANES)
        spread_o[:, across] = res[1, c * tall : (c + 1) * tall].astype(F32) * scale
        for k in range(tall // LANES):
            at = c * tall + k * LANES
            merge_o[across, k * LANES : (k + 1) * LANES] = (
                res[0, at : at + LANES].astype(F32) * scale
            ).T
    opened = jax.nn.sigmoid(gate[...])
    opened = opened * (1.0 - opened) * scale
    for h in range(2):
        at = slice(h * units, (h + 1) * units)
        bias_o[:, at] = vec[h : h + 1, :units] * (0.25 * scale)
        gate_o[:, at] = vec[2 + h : 3 + h, :units] * opened[:, at]


def on_device(tokens, out_grad, spread_weight, merge_weight, switch_bias, gate_logit):
    n = lax.axis_size("seq")
    rows, units = tokens.shape
    switch, hidden_size = spread_weight.shape
    half = rows // 2
    wide_units = rounded_up(units)
    others = n // (2 * GROUP)
    more = max(others - 1, 1)
    flat_rows = switch * hidden_size // LANES
    quarter = flat_rows // SIDE
    piece = quarter // SIDE
    vec_shape = (4, wide_units)
    any_spec = pl.BlockSpec(memory_space=pl.ANY)
    vmem_spec = pl.BlockSpec(memory_space=pltpu.VMEM)
    dma = pltpu.SemaphoreType.DMA
    vmem = pltpu.VMEM
    gate_row = gate_logit.reshape(1, switch)
    net, tg, res, vec = pl.pallas_call(
        functools.partial(step_kernel, n),
        out_shape=(
            jax.ShapeDtypeStruct((rows, units), BF16),
            jax.ShapeDtypeStruct((rows, units), BF16),
            jax.ShapeDtypeStruct((2, flat_rows, LANES), BF16),
            jax.ShapeDtypeStruct(vec_shape, F32),
        ),
        in_specs=[any_spec] * 6,
        out_specs=(vmem_spec,) * 4,
        scratch_shapes=[
            vmem((switch, hidden_size), BF16),
            vmem((hidden_size, switch), BF16),
            vmem((1, switch), F32),
            vmem((1, switch), F32),
            vmem((rows, units), BF16),
            vmem((rows, units), BF16),
            vmem((rows, units), BF16),
            vmem((rows, units), BF16),
            vmem((rows, wide_units), BF16),
            vmem((2, wide_units, hidden_size), BF16),
            vmem((2, hidden_size, wide_units), BF16),
            vmem((2, hidden_size, wide_units), BF16),
            vmem((2, wide_units, hidden_size), BF16),
            vmem((8, wide_units), F32),
            vmem((2, SECTIONS, 2, half, wide_units), BF16),
            vmem((2, SECTIONS, half, hidden_size), BF16),
            vmem((SECTIONS, 2, half, wide_units), BF16),
            vmem((SECTIONS, half, hidden_size), BF16),
            vmem((half, hidden_size), F32),
            vmem((SECTIONS, half, hidden_size), F32),
            vmem((SECTIONS, half, hidden_size), F32),
            vmem((SECTIONS, half, LANES), F32),
            vmem((flat_rows, LANES), F32),
            vmem((flat_rows, LANES), BF16),
            vmem((quarter, LANES), F32),
            vmem((quarter, LANES), BF16),
            vmem((SIDE - 1, quarter, LANES), BF16),
            vmem((SIDE - 1, piece, LANES), BF16),
            vmem((more, piece, LANES), BF16),
            vmem((piece, LANES), BF16),
            vmem((4, 8, wide_units), F32),
            vmem(vec_shape, F32),
            vmem(vec_shape, F32),
            vmem(vec_shape, F32),
            vmem(vec_shape, F32),
            vmem(vec_shape, F32),
            vmem((SIDE - 1,) + vec_shape, F32),
            vmem((SIDE - 1,) + vec_shape, F32),
            vmem((more,) + vec_shape, F32),
            dma((6,)),
            dma((4, GROUP, 2)),
            dma((2, SECTIONS, 2)),
            dma((SIDE, 2)),
            dma((SIDE, 2)),
            dma((more + 1, 2)),
            dma((SIDE, 2)),
            dma((SIDE, 2)),
            dma((SIDE, 2)),
            dma((2,)),
            dma((SIDE, 2)),
            dma((SIDE, 2)),
            dma((more + 1, 2)),
        ],
        compiler_params=pltpu.CompilerParams(
            collective_id=0, has_side_effects=True, vmem_limit_bytes=48 * 2**20
        ),
        name="switch_step",
    )(tokens, out_grad, spread_weight, merge_weight, switch_bias.reshape(1, switch), gate_row)
    scale = 1.0 / math.sqrt(n * rows)
    net, tg, spread, merge, bias, gate = pl.pallas_call(
        functools.partial(finish_kernel, scale),
        out_shape=(
            jax.ShapeDtypeStruct((rows, units), BF16),
            jax.ShapeDtypeStruct((rows, units), BF16),
            jax.ShapeDtypeStruct((switch, hidden_size), F32),
            jax.ShapeDtypeStruct((hidden_size, switch), F32),
            jax.ShapeDtypeStruct((1, switch), F32),
            jax.ShapeDtypeStruct((1, switch), F32),
        ),
        in_specs=[vmem_spec] * 5,
        out_specs=(vmem_spec,) * 6,
        compiler_params=pltpu.CompilerParams(vmem_limit_bytes=32 * 2**20),
        name="finish",
    )(res, net, tg, vec, gate_row)
    return net, tg, spread, merge, bias.reshape(switch), gate.reshape(switch)


def solution(mesh):
    placed = (P("seq", None), P("seq", None), P(), P(), P(), P())
    return jax.shard_map(
        on_device,
        mesh=mesh,
        in_specs=placed,
        out_specs=placed,
        check_vma=False,
    )
```

time: 260 us -> 77.6 us (0.30)
  waiting for transfers between devices: 134 us -> 0 us
  Pallas kernels: 0 us -> 69.3 us
  blocking collectives: 40.1 us -> 0 us
  starting transfers between devices: 28 us -> 0 us
  matrix products: 19.2 us -> 0 us
  between operations: 15.5 us -> 0.68 us
  other arithmetic: 11.5 us -> 1.19 us
  local copies, waits for them, and re-layouts: 11.6 us -> 6.21 us
    psum x1 -> x0, waiting for transfers between devices: 108 us -> none  [on_device(): lax.psum((spread_total, merge_total, bias_total, gate_total), 'seq')]
    pallas_call x0 -> x2, Pallas kernels: none -> 69.3 us  [the longest x1 67.4 us: on_device(): pl.pallas_call(functools.partial(step_kernel, n), out_shape=(jax.ShapeDty...]
    psum x1 -> x0, blocking collectives: 40.1 us -> none  [on_device(): lax.psum((spread_total, merge_total, bias_total, gate_total), 'seq')]
    ppermute x16 -> x0, starting transfers between devices: 28 us -> none  [swapped(): return lax.ppermute(value, axis, pairs)]
    ppermute x16 -> x0, waiting for transfers between devices: 25.6 us -> none  [swapped(): return lax.ppermute(value, axis, pairs)]
    dot_general x24 -> x0, matrix products: 19.2 us -> none  [the longest x4 5.39 us: switch_backward(): lax.dot_general(hidden, masked_branch, (((0,), (0,)), ((), ())), preferre...]
    mul x4 -> x0, other arithmetic: 5.4 us -> none  [the longest x1 2.46 us: on_device(): merge_sum * grad_scale]
    unnamed x88 -> x8, local copies, waits for them, and re-layouts: 6.56 us -> 4.78 us
  transfers between devices with their start and end apart: 17 -> 0, of which waited for: 13 -> 0; matrix products, arithmetic and copies ran while one was open for 3% -> 0% of each run, Pallas kernels for 0% -> 0%
where the time goes in v1:
time: 77.6 us; the launch traced here: 77.4 us
  Pallas kernels  69.3 us (89%)
  local copies, waits for them, and re-layouts  6.21 us (8%)
  other arithmetic  1.19 us (2%)
    pallas_call x1, Pallas kernels, on_device(): pl.pallas_call(functools.partial(step_kernel, n), out_shape=(jax.ShapeDty...  67.4 us
    unnamed x8, local copies, waits for them, and re-layouts  4.78 us
    pallas_call x1, Pallas kernels, on_device(): pl.pallas_call(functools.partial(finish_kernel, scale), out_shape=(jax.Sh...  1.86 us

profile of v1, /device:TPU:0, one launch (start us, length us, event | category | flops | bytes accessed | tf_op | source)
XLA Modules:
  0.0 77.4 jit_solution(6721767224482258332)
XLA Ops:
  0.6 0.0 copy-start
  0.6 0.7 reshape.25.gate
  1.4 0.7 reshape.24.bias
  2.1 1.1 %copy.12.tok = bf16[512,192]{1,0:T(8,128)(2,1)S(1)} copy(bf16[512,192]{0,1:T(8,128)(2,1)} %param.6) | data formatting | bytes 393216 | tf_op args[0]
  3.1 1.1 %copy.13.og = bf16[512,192]{1,0:T(8,128)(2,1)S(1)} copy(bf16[512,192]{0,1:T(8,128)(2,1)} %param.7) | data formatting | bytes 393216 | tf_op args[1]
  4.2 0.0 copy-done
  4.2 0.0 copy-start.1
  4.2 1.1 %copy-done.1 = bf16[768,384]{1,0:T(8,128)(2,1)S(1)} copy-done((bf16[768,384]{1,0:T(8,128)(2,1)S(1)}, bf16[768,384]{1,0:T(8,128)(2,1)}, u32[]{:S(2)}) %copy-start.1) | copy-done | bytes 589848
  5.3 67.4 %switch_step.1 = (bf16[512,192]{1,0:T(8,128)(2,1)S(1)}, bf16[512,192]{1,0:T(8,128)(2,1)S(1)}, bf16[2,2304,128]{2,1,0:T(8,128)(2,1)S(1)}, f32[4,256]{1,0:T(4,128)S(1)}) custom-call(bf16[512,192]{1,0:T(8,128)(2,1)S(1)} %copy.12.tok, bf16[512,192]{1,0:T(8,128)(2,1)S(1)} %copy.13.og, bf16[384,768]{1,0:T(8,128)(2,1)S(1)} %copy-done, ...), custom_call_target="tpu_custom_call" | custom-call | tf_op jit(solution)/shard_map/switch_step/pallas_call | solution.py:413
  72.7 1.9 %finish.1 = (bf16[512,192]{1,0:T(8,128)(2,1)S(1)}, bf16[512,192]{1,0:T(8,128)(2,1)S(1)}, f32[384,768]{1,0:T(8,128)}, f32[768,384]{1,0:T(8,128)}, f32[1,384]{1,0:T(1,128)S(1)}, /*index=5*/f32[1,384]{1,0:T(1,128)S(1)}) custom-call(bf16[2,2304,128]{2,1,0:T(8,128)(2,1)S(1)} %get-tuple-element.16.res, bf16[512,192]{1,0:T(8,128)(2,1)S(1)} %get-tuple-element.17.net, ...), custom_call_target="tpu_custom_call" | custom-call | tf_op jit(solution)/shard_map/finish/pallas_call | solution.py:483
  74.6 0.8 %copy.14 = bf16[512,192]{0,1:T(8,128)(2,1)} copy(bf16[512,192]{1,0:T(8,128)(2,1)S(1)} %get-tuple-element.26) | data formatting | bytes 393216
  75.4 0.6 reduce
  76.0 0.6 reduce.1
  76.6 0.8 %copy.15 = bf16[512,192]{0,1:T(8,128)(2,1)} copy(bf16[512,192]{1,0:T(8,128)(2,1)S(1)} %get-tuple-element.27) | data formatting | bytes 393216
Async XLA Ops:
  0.6 3.6 %copy-start = (bf16[384,768]{1,0:T(8,128)(2,1)S(1)}, bf16[384,768]{1,0:T(8,128)(2,1)}, u32[]{:S(2)}) copy-start(bf16[384,768]{1,0:T(8,128)(2,1)} %sw.1) | copy-start | bytes 1769476
  4.2 1.1 %copy-start.1 = (bf16[768,384]{1,0:T(8,128)(2,1)S(1)}, bf16[768,384]{1,0:T(8,128)(2,1)}, u32[]{:S(2)}) copy-start(bf16[768,384]{1,0:T(8,128)(2,1)} %mw.1) | copy-start | bytes 1769476

commit v2 on v1

--- a/solution.py
+++ b/solution.py
@@ -16,12 +16,23 @@
 F32 = jnp.float32
 BF16 = jnp.bfloat16
 
-sqrt_half = 0.7071067811865476
+log2_e = 1.4426950408889634
 inv_sqrt_two_pi = 0.3989422804014327
 
 
 def dot(a, b):
     return jnp.dot(a, b, preferred_element_type=F32)
+
+
+def distribution(value, bell):
+    base = 1.0 + (0.3275911 * 0.7071067811865476) * jnp.abs(value)
+    guess = pl.reciprocal(base, approx=True)
+    t = guess * (2.0 - base * guess)
+    tail = 0.5 * 1.061405429
+    for factor in (-1.453152027, 1.421413741, -0.284496736, 0.254829592):
+        tail = tail * t + 0.5 * factor
+    tail = tail * t * bell
+    return jnp.where(value < 0.0, tail, 1.0 - tail)
 
 
 def rounded_up(size):
@@ -33,7 +44,7 @@
     tok, og, sw, mw, bias, gate,
     net_o, tg_o, res, vec_o,
     sw_v, mw_v, bias_v, gate_v,
-    xin, gin, xs, gs,
+    xt, gt, tok_v, og_v, xin, gin, xs, gs,
     state, wp, wt, mp, mt, rows_v,
     sides, wides, r_sides, r_wides,
     pre, normed, slope, inv,
@@ -73,8 +84,8 @@
         )
 
     loads = [
-        pltpu.make_async_copy(tok.at[pl.ds(top * sub, sub)], xin.at[pl.ds(top * sub, sub)], load_sem.at[0]),
-        pltpu.make_async_copy(og.at[pl.ds(top * sub, sub)], gin.at[pl.ds(top * sub, sub)], load_sem.at[1]),
+        pltpu.make_async_copy(tok, xt, load_sem.at[0]),
+        pltpu.make_async_copy(og, gt, load_sem.at[1]),
         pltpu.make_async_copy(sw, sw_v, load_sem.at[2]),
         pltpu.make_async_copy(mw, mw_v, load_sem.at[3]),
         pltpu.make_async_copy(bias, bias_v, load_sem.at[4]),
@@ -94,6 +105,13 @@
         pl.semaphore_signal(
             barrier, inc=1, device_id=(mid_dev((mid + j) % others),), device_id_type=MESH
         )
+    own = pl.ds(pl.multiple_of(top * sub, sub), sub)
+    loads[0].wait()
+    tok_v[...] = xt[...].T
+    xin[own] = tok_v[own]
+    loads[1].wait()
+    og_v[...] = gt[...].T
+    gin[own] = og_v[own]
     pl.semaphore_wait(barrier, GROUP + others - 1)
 
     def exchange(src, dst, number):
@@ -121,8 +139,8 @@
 
         return start, received, sent
 
-    tok_start, tok_received, tok_sent = exchange(tok, xin, 0)
-    og_start, og_received, og_sent = exchange(og, gin, 1)
+    tok_start, tok_received, tok_sent = exchange(tok_v, xin, 0)
+    og_start, og_received, og_sent = exchange(og_v, gin, 1)
     net_start, net_received, net_sent = exchange(xs, net_o, 2)
     tg_start, tg_received, tg_sent = exchange(gs, tg_o, 3)
     tok_start()
@@ -143,8 +161,8 @@
     loads[5].wait()
     rows_v[...] = jnp.zeros(rows_v.shape, F32)
     for h in range(2):
-        rows_v[h : h + 1, :units] = jax.nn.sigmoid(gate_v[:, h * units : (h + 1) * units])
-        rows_v[2 + h : 3 + h, :units] = bias_v[:, h * units : (h + 1) * units]
+        rows_v[h : h + 1, :units] = jax.nn.sigmoid(gate_v[...].reshape(1, -1)[:, h * units : (h + 1) * units])
+        rows_v[2 + h : 3 + h, :units] = bias_v[...].reshape(1, -1)[:, h * units : (h + 1) * units]
     sums[...] = jnp.zeros(sums.shape, F32)
     state[...] = jnp.zeros(state.shape, BF16)
 
@@ -156,7 +174,6 @@
                 yield h, slice(k * length, (k + 1) * length), slice(at, at + length)
 
     chunk = 32
-    loads[0].wait()
     tok_received()
     state[:, :units] = xin[...]
     for s in range(SECTIONS):
@@ -171,10 +188,11 @@
             centered = value - jnp.mean(value, -1, keepdims=True)
             scale = lax.rsqrt(jnp.mean(centered * centered, -1, keepdims=True) + 1e-05)
             value = centered * scale
-            phi_sum = 0.5 * (1.0 + lax.erf(value * sqrt_half))
+            bell = jnp.exp2(value * value * (-0.5 * log2_e))
+            phi_sum = distribution(value, bell)
             wides[0, s, at] = (value * phi_sum).astype(BF16)
             normed[s, at] = value
-            slope[s, at] = phi_sum + value * jnp.exp(-0.5 * value * value) * inv_sqrt_two_pi
+            slope[s, at] = phi_sum + value * bell * inv_sqrt_two_pi
             inv[s, at] = jnp.broadcast_to(scale, (chunk, LANES))
 
         outs = [
@@ -190,7 +208,7 @@
             else:
                 xs[outer] = outs[h][inner, :units]
     net_start()
-    net_o[pl.ds(top * sub, sub)] = xs[pl.ds(top * sub, sub)]
+    net_o[own] = xs[own]
 
     def gather_grads(side, wide, first):
         for h in range(2):
@@ -207,7 +225,6 @@
         ]
 
     vec_mate = remote(v0, rvm, vm_sem, mate)
-    loads[1].wait()
     og_received()
     state[:, :units] = gin[...]
     for s in reversed(range(SECTIONS)):
@@ -252,7 +269,7 @@
                 gs[outer] = value[:, :units]
         if s == 0:
             tg_start()
-            tg_o[pl.ds(top * sub, sub)] = gs[pl.ds(top * sub, sub)]
+            tg_o[own] = gs[own]
         gather_grads(sides.at[core, s], wides.at[core, s], s == SECTIONS - 1)
         if s < SECTIONS - 1:
             for copy in mate_copies(s + 1):
@@ -375,8 +392,8 @@
 def finish_kernel(scale, res, net, tg, vec, gate, net_o, tg_o, spread_o, merge_o, bias_o, gate_o):
     units = net.shape[1]
     tall, wide = spread_o.shape
-    net_o[...] = net[...]
-    tg_o[...] = tg[...]
+    net_o[...] = net[...].T
+    tg_o[...] = tg[...].T
     for c in range(wide // LANES):
         across = slice(c * LANES, (c + 1) * LANES)
         spread_o[:, across] = res[1, c * tall : (c + 1) * tall].astype(F32) * scale
@@ -387,10 +404,11 @@
             ).T
     opened = jax.nn.sigmoid(gate[...])
     opened = opened * (1.0 - opened) * scale
-    for h in range(2):
-        at = slice(h * units, (h + 1) * units)
-        bias_o[:, at] = vec[h : h + 1, :units] * (0.25 * scale)
-        gate_o[:, at] = vec[2 + h : 3 + h, :units] * opened[:, at]
+    both = [
+        jnp.concatenate([vec[r : r + 1, :units], vec[r + 1 : r + 2, :units]], 1) for r in (0, 2)
+    ]
+    bias_o[...] = both[0].reshape(-1) * (0.25 * scale)
+    gate_o[...] = both[1].reshape(-1) * opened
 
 
 def on_device(tokens, out_grad, spread_weight, merge_weight, switch_bias, gate_logit):
@@ -405,11 +423,10 @@
     quarter = flat_rows // SIDE
     piece = quarter // SIDE
     vec_shape = (4, wide_units)
-    any_spec = pl.BlockSpec(memory_space=pl.ANY)
+    any_spec = pl.BlockSpec(memory_space=pltpu.HBM)
     vmem_spec = pl.BlockSpec(memory_space=pltpu.VMEM)
     dma = pltpu.SemaphoreType.DMA
     vmem = pltpu.VMEM
-    gate_row = gate_logit.reshape(1, switch)
     net, tg, res, vec = pl.pallas_call(
         functools.partial(step_kernel, n),
         out_shape=(
@@ -423,8 +440,12 @@
         scratch_shapes=[
             vmem((switch, hidden_size), BF16),
             vmem((hidden_size, switch), BF16),
-            vmem((1, switch), F32),
-            vmem((1, switch), F32),
+            vmem((switch,), F32),
+            vmem((switch,), F32),
+            vmem((units, rows), BF16),
+            vmem((units, rows), BF16),
+            vmem((rows, units), BF16),
+            vmem((rows, units), BF16),
             vmem((rows, units), BF16),
             vmem((rows, units), BF16),
             vmem((rows, units), BF16),
@@ -478,24 +499,24 @@
             collective_id=0, has_side_effects=True, vmem_limit_bytes=48 * 2**20
         ),
         name="switch_step",
-    )(tokens, out_grad, spread_weight, merge_weight, switch_bias.reshape(1, switch), gate_row)
+    )(tokens.T, out_grad.T, spread_weight, merge_weight, switch_bias, gate_logit)
     scale = 1.0 / math.sqrt(n * rows)
     net, tg, spread, merge, bias, gate = pl.pallas_call(
         functools.partial(finish_kernel, scale),
         out_shape=(
-            jax.ShapeDtypeStruct((rows, units), BF16),
-            jax.ShapeDtypeStruct((rows, units), BF16),
+            jax.ShapeDtypeStruct((units, rows), BF16),
+            jax.ShapeDtypeStruct((units, rows), BF16),
             jax.ShapeDtypeStruct((switch, hidden_size), F32),
             jax.ShapeDtypeStruct((hidden_size, switch), F32),
-            jax.ShapeDtypeStruct((1, switch), F32),
-            jax.ShapeDtypeStruct((1, switch), F32),
+            jax.ShapeDtypeStruct((switch,), F32),
+            jax.ShapeDtypeStruct((switch,), F32),
         ),
         in_specs=[vmem_spec] * 5,
         out_specs=(vmem_spec,) * 6,
         compiler_params=pltpu.CompilerParams(vmem_limit_bytes=32 * 2**20),
         name="finish",
-    )(res, net, tg, vec, gate_row)
-    return net, tg, spread, merge, bias.reshape(switch), gate.reshape(switch)
+    )(res, net, tg, vec, gate_logit)
+    return net.T, tg.T, spread, merge, bias, gate
 
 
 def solution(mesh):

time: 77.6 us -> 77.6 us (level)
  Pallas kernels: 69.3 us -> 71.3 us
  other arithmetic: 1.19 us -> 0 us
  local copies, waits for them, and re-layouts: 6.21 us -> 5.34 us
    pallas_call x1, Pallas kernels: 67.4 us -> 69.4 us  [on_device(): pl.pallas_call(functools.partial(step_kernel, n), out_shape=(jax.ShapeDty...]
    reshape x2 -> x0, local copies, waits for them, and re-layouts: 1.43 us -> none  [the longest x1 0.74 us: on_device(): gate_row = gate_logit.reshape(1, switch)]
    pallas_call x2 -> x0, other arithmetic: 1.19 us -> none  [on_device(): pl.pallas_call(functools.partial(finish_kernel, scale), out_shape=(jax.Sh...]
    unnamed x8 -> x12, local copies, waits for them, and re-layouts: 4.78 us -> 5.34 us
where the time goes in v2:
time: 77.6 us; the launch traced here: 77.3 us
  Pallas kernels  71.3 us (92%)
  local copies, waits for them, and re-layouts  5.34 us (7%)
    pallas_call x1, Pallas kernels, on_device(): pl.pallas_call(functools.partial(step_kernel, n), out_shape=(jax.ShapeDty...  69.4 us
    unnamed x12, local copies, waits for them, and re-layouts  5.34 us
    pallas_call x1, Pallas kernels, on_device(): pl.pallas_call(functools.partial(finish_kernel, scale), out_shape=(jax.Sh...  1.95 us

profile of v2, /device:TPU:0, one launch (start us, length us, event | category | flops | bytes accessed | tf_op | source)
XLA Modules:
  0.0 77.3 jit_solution(13776712858088170586)
XLA Ops:
  0.6 0.0 copy-start
  0.6 1.1 %copy-done = bf16[384,768]{1,0:T(8,128)(2,1)S(1)} copy-done((bf16[384,768]{1,0:T(8,128)(2,1)S(1)}, bf16[384,768]{1,0:T(8,128)(2,1)}, u32[]{:S(2)}) %copy-start) | copy-done | bytes 589848
  1.7 0.0 copy-start.1
  1.7 1.1 %copy-done.1 = bf16[768,384]{1,0:T(8,128)(2,1)S(1)} copy-done((bf16[768,384]{1,0:T(8,128)(2,1)S(1)}, bf16[768,384]{1,0:T(8,128)(2,1)}, u32[]{:S(2)}) %copy-start.1) | copy-done | bytes 589848
  2.8 0.0 copy-start.2
  2.8 0.9 %copy-done.2 = bf16[512,192]{0,1:T(8,128)(2,1)S(1)} copy-done((bf16[512,192]{0,1:T(8,128)(2,1)S(1)}, bf16[512,192]{0,1:T(8,128)(2,1)}, u32[]{:S(2)}) %copy-start.2) | copy-done | bytes 196632
  3.7 0.0 copy-start.3
  3.7 0.9 %copy-done.3 = bf16[512,192]{0,1:T(8,128)(2,1)S(1)} copy-done((bf16[512,192]{0,1:T(8,128)(2,1)S(1)}, bf16[512,192]{0,1:T(8,128)(2,1)}, u32[]{:S(2)}) %copy-start.3) | copy-done | bytes 196632
  4.6 0.0 copy-start.4
  4.6 0.7 copy-done.4
  5.3 0.0 copy-start.5
  5.3 0.7 copy-done.5
  6.0 69.4 %switch_step.1 = (bf16[512,192]{1,0:T(8,128)(2,1)S(1)}, bf16[512,192]{1,0:T(8,128)(2,1)S(1)}, bf16[2,2304,128]{2,1,0:T(8,128)(2,1)S(1)}, f32[4,256]{1,0:T(4,128)S(1)}) custom-call(bf16[192,512]{1,0:T(8,128)(2,1)S(1)} %bitcast.4, bf16[192,512]{1,0:T(8,128)(2,1)S(1)} %bitcast.5, bf16[384,768]{1,0:T(8,128)(2,1)S(1)} %copy-done, bf16[768,384]{1,0:T(8,128)(2,1)S(1)} %copy-done.1, ...), custom_call_target="tpu_custom_call" | custom-call | tf_op jit(solution)/shard_map/switch_step/pallas_call | solution.py:430
  75.4 1.9 %finish.1 = (bf16[192,512]{1,0:T(8,128)(2,1)}, bf16[192,512]{1,0:T(8,128)(2,1)}, f32[384,768]{1,0:T(8,128)}, f32[768,384]{1,0:T(8,128)}, f32[384]{0:T(512)}, /*index=5*/f32[384]{0:T(512)}) custom-call(bf16[2,2304,128]{2,1,0:T(8,128)(2,1)S(1)} %get-tuple-element.16.res, bf16[512,192]{1,0:T(8,128)(2,1)S(1)} %get-tuple-element.17.net, ...), custom_call_target="tpu_custom_call" | custom-call | tf_op jit(solution)/shard_map/finish/pallas_call | solution.py:504
Async XLA Ops:
  0.6 1.1 %copy-start = (bf16[384,768]{1,0:T(8,128)(2,1)S(1)}, bf16[384,768]{1,0:T(8,128)(2,1)}, u32[]{:S(2)}) copy-start(bf16[384,768]{1,0:T(8,128)(2,1)} %sw.1) | copy-start | bytes 1769476
  1.7 1.1 %copy-start.1 = (bf16[768,384]{1,0:T(8,128)(2,1)S(1)}, bf16[768,384]{1,0:T(8,128)(2,1)}, u32[]{:S(2)}) copy-start(bf16[768,384]{1,0:T(8,128)(2,1)} %mw.1) | copy-start | bytes 1769476
  2.8 0.9 %copy-start.2 = (bf16[512,192]{0,1:T(8,128)(2,1)S(1)}, bf16[512,192]{0,1:T(8,128)(2,1)}, u32[]{:S(2)}) copy-start(bf16[512,192]{0,1:T(8,128)(2,1)} %param.6) | copy-start | bytes 589828
  3.7 0.9 %copy-start.3 = (bf16[512,192]{0,1:T(8,128)(2,1)S(1)}, bf16[512,192]{0,1:T(8,128)(2,1)}, u32[]{:S(2)}) copy-start(bf16[512,192]{0,1:T(8,128)(2,1)} %param.7) | copy-start | bytes 589828
  4.6 0.7 copy-start.4
  5.3 0.7 copy-start.5

commit v3 on v2

--- a/solution.py
+++ b/solution.py
@@ -59,7 +59,9 @@
     hidden_size = sw_v.shape[1]
     stride = n // GROUP
     others = n // (2 * GROUP)
-    quarter = flat.shape[0] // SIDE
+    blocks = rv1.shape[0]
+    block_rows = flat.shape[0] // blocks
+    quarter = block_rows // SIDE
     piece = quarter // SIDE
 
     me = lax.axis_index("seq")
@@ -144,7 +146,6 @@
     net_start, net_received, net_sent = exchange(xs, net_o, 2)
     tg_start, tg_received, tg_sent = exchange(gs, tg_o, 3)
     tok_start()
-    og_start()
 
     pad = wp.shape[1] - units
     loads[2].wait()
@@ -173,15 +174,16 @@
                 at = (2 * k + h) * length
                 yield h, slice(k * length, (k + 1) * length), slice(at, at + length)
 
-    chunk = 32
+    chunk = 16
     tok_received()
+    og_start()
     state[:, :units] = xin[...]
     for s in range(SECTIONS):
         for h, inner, outer in spans(s):
             sides[1, s, h, inner] = state[outer]
         pre[...] = dot(sides[1, s, 0], wp[0]) + dot(sides[1, s, 1], wp[1])
 
-        @pl.loop(0, half // chunk)
+        @pl.loop(0, half // chunk, unroll=4)
         def _(i):
             at = pl.ds(pl.multiple_of(i * chunk, chunk), chunk)
             value = pre[at]
@@ -210,13 +212,22 @@
     net_start()
     net_o[own] = xs[own]
 
-    def gather_grads(side, wide, first):
-        for h in range(2):
-            term = dot(side[h].T[:units], wide[...])
-            for c in range(hidden_size // LANES):
-                at = slice((2 * c + h) * units, (2 * c + h + 1) * units)
-                block = term[:, c * LANES : (c + 1) * LANES]
-                flat[at] = block if first else flat[at] + block
+    def gather_grads(pairs, first=False, only=None):
+        turned = [[side[h].T[:units] for h in range(2)] for side, _ in pairs]
+        width = hidden_size // blocks
+        for b in range(blocks):
+            for h in range(2):
+                term = sum(
+                    dot(turned[k][h], wide[:, b * width : (b + 1) * width])
+                    for k, (_, wide) in enumerate(pairs)
+                )
+                for c in range(width // LANES):
+                    at = b * block_rows + (2 * c + h) * units
+                    at = slice(at, at + units)
+                    block = term[:, c * LANES : (c + 1) * LANES]
+                    flat[at] = block if first else flat[at] + block
+            if only is not None:
+                only(b)
 
     def mate_copies(s):
         return [
@@ -242,7 +253,7 @@
                 v0[r : r + 1] = jnp.sum(sums[r], 0, keepdims=True)
             vec_mate.start()
 
-        @pl.loop(0, half // chunk)
+        @pl.loop(0, half // chunk, unroll=4)
         def _(i):
             at = pl.ds(pl.multiple_of(i * chunk, chunk), chunk)
             value = normed[s, at]
@@ -270,104 +281,126 @@
         if s == 0:
             tg_start()
             tg_o[own] = gs[own]
-        gather_grads(sides.at[core, s], wides.at[core, s], s == SECTIONS - 1)
-        if s < SECTIONS - 1:
+        own_pair = (sides.at[core, s], wides.at[core, s])
+        if s == SECTIONS - 1:
+            gather_grads([own_pair], True)
+        else:
             for copy in mate_copies(s + 1):
                 copy.wait_recv()
-            gather_grads(r_sides.at[s + 1], r_wides.at[s + 1], False)
+            gather_grads([own_pair, (r_sides.at[s + 1], r_wides.at[s + 1])])
+
+    def rows_at(b, first, size):
+        return pl.ds(pl.multiple_of(b * block_rows + first, 16), size)
+
+    def first_copy(b, j):
+        to = (col + j) % SIDE
+        return remote(
+            flat_b.at[rows_at(b, to * quarter, quarter)], rv1.at[b, j - 1],
+            rs1_sem.at[b, j], dev(line * SIDE + to),
+        )
+
+    def second_copy(b, j):
+        to = (line + j) % SIDE
+        return remote(
+            part_b.at[b, pl.ds(pl.multiple_of(to * piece, piece), piece)], rv2.at[b, j - 1],
+            rs2_sem.at[b, j], dev(to * SIDE + col),
+        )
+
+    def other_copy(b, j):
+        return remote(
+            last.at[b], rvx.at[b, j - 1], rsx_sem.at[b, j], mid_dev((mid + j) % others)
+        )
+
+    def line_copy(b, j):
+        span = res.at[core, rows_at(b, col * quarter + line * piece, piece)]
+        return remote(span, span, ag2_sem.at[b, j], dev((line + j) % SIDE * SIDE + col))
+
+    def col_copy(b, j):
+        span = res.at[core, rows_at(b, col * quarter, quarter)]
+        return remote(span, span, ag1_sem.at[b, j], dev(line * SIDE + (col + j) % SIDE))
+
+    def mate_copy(b, j):
+        at = (col + SIDE - j) % SIDE
+        span = res.at[core, rows_at(b, at * quarter, quarter)]
+        return remote(span, span, fwd_sem.at[b, j], mate)
+
+    def vec_first(j):
+        return remote(v1, rvv1.at[j - 1], vv1_sem.at[j], dev(line * SIDE + (col + j) % SIDE))
+
+    def vec_second(j):
+        return remote(v2, rvv2.at[j - 1], vv2_sem.at[j], dev((line + j) % SIDE * SIDE + col))
+
+    def vec_other(j):
+        return remote(v3, rvvx.at[j - 1], vvx_sem.at[j], mid_dev((mid + j) % others))
+
+    peers = range(1, SIDE)
+
+    def send_block(b):
+        at = slice(b * block_rows, (b + 1) * block_rows)
+        flat_b[at] = flat[at].astype(BF16)
+        for j in peers:
+            first_copy(b, j).start()
+
+    vec_mate.wait_recv()
+    v1[...] = v0[...] + rvm[...]
+    for j in peers:
+        vec_first(j).start()
     for copy in mate_copies(0):
         copy.wait_recv()
-    gather_grads(r_sides.at[0], r_wides.at[0], False)
-    flat_b[...] = flat[...].astype(BF16)
-
-    def first_copies(j):
-        to = (col + j) % SIDE
-        target = dev(line * SIDE + to)
-        return [
-            remote(flat_b.at[pl.ds(to * quarter, quarter)], rv1.at[j - 1], rs1_sem.at[j], target),
-            remote(v1, rvv1.at[j - 1], vv1_sem.at[j], target),
-        ]
-
-    def second_copies(j):
-        to = (line + j) % SIDE
-        target = dev(to * SIDE + col)
-        return [
-            remote(part_b.at[pl.ds(to * piece, piece)], rv2.at[j - 1], rs2_sem.at[j], target),
-            remote(v2, rvv2.at[j - 1], vv2_sem.at[j], target),
-        ]
-
-    def other_copies(j):
-        target = mid_dev((mid + j) % others)
-        return [
-            remote(last, rvx.at[j - 1], rsx_sem.at[j], target),
-            remote(v3, rvvx.at[j - 1], vvx_sem.at[j], target),
-        ]
-
-    for j in range(1, SIDE):
-        first_copies(j)[0].start()
-    vec_mate.wait_recv()
-    v1[...] = v0[...] + rvm[...]
-    for j in range(1, SIDE):
-        first_copies(j)[1].start()
-    for j in range(1, SIDE):
-        for copy in first_copies(j):
-            copy.wait_recv()
-    total = flat[pl.ds(pl.multiple_of(col * quarter, quarter), quarter)]
-    for j in range(SIDE - 1):
-        total = total + rv1[j].astype(F32)
-    part[...] = total
-    part_b[...] = total.astype(BF16)
-    v2[...] = v1[...] + rvv1[0] + rvv1[1] + rvv1[2]
-    for j in range(1, SIDE):
-        for copy in second_copies(j):
-            copy.start()
-    for j in range(1, SIDE):
-        for copy in second_copies(j):
-            copy.wait_recv()
-    total = part[pl.ds(pl.multiple_of(line * piece, piece), piece)]
-    for j in range(SIDE - 1):
-        total = total + rv2[j].astype(F32)
+    gather_grads([(r_sides.at[0], r_wides.at[0])], only=send_block)
+    for b in range(blocks):
+        for j in peers:
+            first_copy(b, j).wait_recv()
+        total = flat[rows_at(b, col * quarter, quarter)]
+        for j in range(SIDE - 1):
+            total = total + rv1[b, j].astype(F32)
+        part[b] = total
+        part_b[b] = total.astype(BF16)
+        for j in peers:
+            second_copy(b, j).start()
+        if b == 0:
+            for j in peers:
+                vec_first(j).wait_recv()
+            v2[...] = v1[...] + rvv1[0] + rvv1[1] + rvv1[2]
+            for j in peers:
+                vec_second(j).start()
+    for b in range(blocks):
+        for j in peers:
+            second_copy(b, j).wait_recv()
+        total = part[b, pl.ds(pl.multiple_of(line * piece, piece), piece)]
+        for j in range(SIDE - 1):
+            total = total + rv2[b, j].astype(F32)
+        if others > 1:
+            last[b] = total.astype(BF16)
+            for j in range(1, others):
+                other_copy(b, j).start()
+            for j in range(1, others):
+                other_copy(b, j).wait_recv()
+                total = total + rvx[b, j - 1].astype(F32)
+        res[core, rows_at(b, col * quarter + line * piece, piece)] = total.astype(BF16)
+        for j in peers:
+            line_copy(b, j).start()
+    for j in peers:
+        vec_second(j).wait_recv()
     vec = v2[...] + rvv2[0] + rvv2[1] + rvv2[2]
     if others > 1:
-        last[...] = total.astype(BF16)
         v3[...] = vec
         for j in range(1, others):
-            for copy in other_copies(j):
-                copy.start()
+            vec_other(j).start()
         for j in range(1, others):
-            for copy in other_copies(j):
-                copy.wait_recv()
-            total = total + rvx[j - 1].astype(F32)
+            vec_other(j).wait_recv()
             vec = vec + rvvx[j - 1]
     vec_o[...] = vec
-    mine = pl.ds(pl.multiple_of(col * quarter + line * piece, piece), piece)
-    res[core, mine] = total.astype(BF16)
-
-    def line_copy(j):
-        to = (line + j) % SIDE
-        return remote(res.at[core, mine], res.at[core, mine], ag2_sem.at[j], dev(to * SIDE + col))
-
-    whole = pl.ds(pl.multiple_of(col * quarter, quarter), quarter)
-
-    def col_copy(j):
-        to = (col + j) % SIDE
-        return remote(res.at[core, whole], res.at[core, whole], ag1_sem.at[j], dev(line * SIDE + to))
-
-    def mate_copy(j):
-        at = (col + SIDE - j) % SIDE
-        span = res.at[core, pl.ds(pl.multiple_of(at * quarter, quarter), quarter)]
-        return remote(span, span, fwd_sem.at[j], mate)
-
-    for j in range(1, SIDE):
-        line_copy(j).start()
-    for j in range(1, SIDE):
-        line_copy(j).wait_recv()
-    for j in range(1, SIDE):
-        col_copy(j).start()
-    mate_copy(0).start()
-    for j in range(1, SIDE):
-        col_copy(j).wait_recv()
-        mate_copy(j).start()
+    for b in range(blocks):
+        for j in peers:
+            line_copy(b, j).wait_recv()
+        for j in peers:
+            col_copy(b, j).start()
+        mate_copy(b, 0).start()
+    for b in range(blocks):
+        for j in peers:
+            col_copy(b, j).wait_recv()
+            mate_copy(b, j).start()
 
     tok_sent()
     og_sent()
@@ -377,16 +410,21 @@
         for copy in mate_copies(s):
             copy.wait_send()
     vec_mate.wait_send()
-    for j in range(1, SIDE):
-        for copy in first_copies(j) + second_copies(j) + [line_copy(j), col_copy(j)]:
-            copy.wait_send()
+    for j in peers:
+        vec_first(j).wait_send()
+        vec_second(j).wait_send()
+        for b in range(blocks):
+            for copy in (first_copy, second_copy, line_copy, col_copy):
+                copy(b, j).wait_send()
     for j in range(1, others):
-        for copy in other_copies(j):
-            copy.wait_send()
+        vec_other(j).wait_send()
+        for b in range(blocks):
+            other_copy(b, j).wait_send()
     net_received()
     tg_received()
-    for j in range(SIDE):
-        mate_copy(j).wait()
+    for b in range(blocks):
+        for j in range(SIDE):
+            mate_copy(b, j).wait()
 
 
 def finish_kernel(scale, res, net, tg, vec, gate, net_o, tg_o, spread_o, merge_o, bias_o, gate_o):
@@ -420,7 +458,8 @@
     others = n // (2 * GROUP)
     more = max(others - 1, 1)
     flat_rows = switch * hidden_size // LANES
-    quarter = flat_rows // SIDE
+    blocks = hidden_size // (2 * LANES)
+    quarter = flat_rows // (blocks * SIDE)
     piece = quarter // SIDE
     vec_shape = (4, wide_units)
     any_spec = pl.BlockSpec(memory_space=pltpu.HBM)
@@ -466,12 +505,12 @@
             vmem((SECTIONS, half, LANES), F32),
             vmem((flat_rows, LANES), F32),
             vmem((flat_rows, LANES), BF16),
-            vmem((quarter, LANES), F32),
-            vmem((quarter, LANES), BF16),
-            vmem((SIDE - 1, quarter, LANES), BF16),
-            vmem((SIDE - 1, piece, LANES), BF16),
-            vmem((more, piece, LANES), BF16),
-            vmem((piece, LANES), BF16),
+            vmem((blocks, quarter, LANES), F32),
+            vmem((blocks, quarter, LANES), BF16),
+            vmem((blocks, SIDE - 1, quarter, LANES), BF16),
+            vmem((blocks, SIDE - 1, piece, LANES), BF16),
+            vmem((blocks, more, piece, LANES), BF16),
+            vmem((blocks, piece, LANES), BF16),
             vmem((4, 8, wide_units), F32),
             vmem(vec_shape, F32),
             vmem(vec_shape, F32),
@@ -484,19 +523,19 @@
             dma((6,)),
             dma((4, GROUP, 2)),
             dma((2, SECTIONS, 2)),
-            dma((SIDE, 2)),
-            dma((SIDE, 2)),
-            dma((more + 1, 2)),
-            dma((SIDE, 2)),
-            dma((SIDE, 2)),
-            dma((SIDE, 2)),
+            dma((blocks, SIDE, 2)),
+            dma((blocks, SIDE, 2)),
+            dma((blocks, more + 1, 2)),
+            dma((blocks, SIDE, 2)),
+            dma((blocks, SIDE, 2)),
+            dma((blocks, SIDE, 2)),
             dma((2,)),
             dma((SIDE, 2)),
             dma((SIDE, 2)),
             dma((more + 1, 2)),
         ],
         compiler_params=pltpu.CompilerParams(
-            collective_id=0, has_side_effects=True, vmem_limit_bytes=48 * 2**20
+            collective_id=0, has_side_effects=True, vmem_limit_bytes=61 * 2**20
         ),
         name="switch_step",
     )(tokens.T, out_grad.T, spread_weight, merge_weight, switch_bias, gate_logit)
@@ -513,7 +552,7 @@
         ),
         in_specs=[vmem_spec] * 5,
         out_specs=(vmem_spec,) * 6,
-        compiler_params=pltpu.CompilerParams(vmem_limit_bytes=32 * 2**20),
+        compiler_params=pltpu.CompilerParams(vmem_limit_bytes=61 * 2**20),
         name="finish",
     )(res, net, tg, vec, gate_logit)
     return net.T, tg.T, spread, merge, bias, gate

time: 77.6 us -> 62.5 us (0.81)
  Pallas kernels: 71.3 us -> 61.7 us
  local copies, waits for them, and re-layouts: 5.34 us -> 0 us
    pallas_call x1, Pallas kernels: 69.4 us -> 58.3 us  [on_device(): pl.pallas_call(functools.partial(step_kernel, n), out_shape=(jax.ShapeDty...]
    unnamed x12 -> x0, local copies, waits for them, and re-layouts: 5.34 us -> none
    pallas_call x1, Pallas kernels: 1.95 us -> 3.34 us  [on_device(): pl.pallas_call(functools.partial(finish_kernel, scale), out_shape=(jax.Sh...]
where the time goes in v3:
time: 62.5 us; the launch traced here: 62.3 us
  Pallas kernels  61.7 us (99%)
  between operations  0.64 us (1%)
    pallas_call x1, Pallas kernels, on_device(): pl.pallas_call(functools.partial(step_kernel, n), out_shape=(jax.ShapeDty...  58.3 us
    pallas_call x1, Pallas kernels, on_device(): pl.pallas_call(functools.partial(finish_kernel, scale), out_shape=(jax.Sh...  3.34 us

profile of v3, /device:TPU:0, one launch (start us, length us, event | category | flops | bytes accessed | tf_op | source)
XLA Modules:
  0.0 62.3 jit_solution(10542911986119118067)
XLA Ops:
  0.6 58.3 %switch_step.1 = (bf16[512,192]{1,0:T(8,128)(2,1)}, bf16[512,192]{1,0:T(8,128)(2,1)}, bf16[2,2304,128]{2,1,0:T(8,128)(2,1)}, f32[4,256]{1,0:T(4,128)}) custom-call(bf16[192,512]{1,0:T(8,128)(2,1)} %bitcast.4, bf16[192,512]{1,0:T(8,128)(2,1)} %bitcast.5, bf16[384,768]{1,0:T(8,128)(2,1)} %sw.1, bf16[768,384]{1,0:T(8,128)(2,1)} %mw.1, f32[384]{0:T(512)} %bias.1, ...), custom_call_target="tpu_custom_call" | custom-call | tf_op jit(solution)/shard_map/switch_step/pallas_call | solution.py:469
  59.0 3.3 %finish.1 = (bf16[192,512]{1,0:T(8,128)(2,1)}, bf16[192,512]{1,0:T(8,128)(2,1)}, f32[384,768]{1,0:T(8,128)}, f32[768,384]{1,0:T(8,128)}, f32[384]{0:T(512)}, /*index=5*/f32[384]{0:T(512)}) custom-call(bf16[2,2304,128]{2,1,0:T(8,128)(2,1)} %get-tuple-element.16.res, bf16[512,192]{1,0:T(8,128)(2,1)} %get-tuple-element.17.net, ...), custom_call_target="tpu_custom_call" | custom-call | tf_op jit(solution)/shard_map/finish/pallas_call | solution.py:543

commit v4 on v3

--- a/solution.py
+++ b/solution.py
@@ -33,6 +33,16 @@
         tail = tail * t + 0.5 * factor
     tail = tail * t * bell
     return jnp.where(value < 0.0, tail, 1.0 - tail)
+
+
+def weave(*tasks):
+    steps = [
+        ((k + 0.5) / len(task), number, step)
+        for number, task in enumerate(tasks)
+        for k, step in enumerate(task)
+    ]
+    for _, _, step in sorted(steps, key=lambda entry: entry[:2]):
+        step()
 
 
 def rounded_up(size):
@@ -167,25 +177,56 @@
     sums[...] = jnp.zeros(sums.shape, F32)
     state[...] = jnp.zeros(state.shape, BF16)
 
-    def spans(section):
-        length = half >> section
+    chains = 2
+    chain_rows = half // chains
+    part_rows = sub // chains
+    chunk = 16
+    width = hidden_size // blocks
+
+    def spans(section, chain):
+        length = chain_rows >> section
         for k in range(2**section):
             for h in range(2):
-                at = (2 * k + h) * length
-                yield h, slice(k * length, (k + 1) * length), slice(at, at + length)
-
-    chunk = 16
-    tok_received()
-    og_start()
-    state[:, :units] = xin[...]
-    for s in range(SECTIONS):
-        for h, inner, outer in spans(s):
-            sides[1, s, h, inner] = state[outer]
-        pre[...] = dot(sides[1, s, 0], wp[0]) + dot(sides[1, s, 1], wp[1])
-
-        @pl.loop(0, half // chunk, unroll=4)
-        def _(i):
-            at = pl.ds(pl.multiple_of(i * chunk, chunk), chunk)
+                at = chain * rows // chains + (2 * k + h) * length
+                inner = chain * chain_rows + k * length
+                yield h, slice(inner, inner + length), slice(at, at + length)
+
+    def rows_of(chain):
+        return slice(chain * chain_rows, (chain + 1) * chain_rows)
+
+    def split_chains(source):
+        for chain in range(chains):
+            for b in range(GROUP):
+                at = (chain * GROUP + b) * part_rows
+                start = b * sub + chain * part_rows
+                state[at : at + part_rows, :units] = source[start : start + part_rows]
+
+    def join_chains(target):
+        for chain in range(chains):
+            for b in range(GROUP):
+                at = (chain * GROUP + b) * part_rows
+                start = b * sub + chain * part_rows
+                target[start : start + part_rows] = state[at : at + part_rows, :units]
+
+    def products(left, weights, at):
+        def one(b):
+            cols = slice(b * width, (b + 1) * width)
+            pre[at, cols] = dot(left[0, at], weights[0, :, cols]) + dot(
+                left[1, at], weights[1, :, cols]
+            )
+
+        return [functools.partial(one, b) for b in range(blocks)]
+
+    def lift(s, chain):
+        def pairs():
+            for h, inner, outer in spans(s, chain):
+                sides[1, s, h, inner] = state[outer]
+
+        return [pairs] + products(sides.at[1, s], wp, rows_of(chain))
+
+    def act(s, chain):
+        def one(i):
+            at = slice(chain * chain_rows + i * chunk, chain * chain_rows + (i + 1) * chunk)
             value = pre[at]
             centered = value - jnp.mean(value, -1, keepdims=True)
             scale = lax.rsqrt(jnp.mean(centered * centered, -1, keepdims=True) + 1e-05)
@@ -197,65 +238,42 @@
             slope[s, at] = phi_sum + value * bell * inv_sqrt_two_pi
             inv[s, at] = jnp.broadcast_to(scale, (chunk, LANES))
 
-        outs = [
-            (
-                rows_v[h : h + 1] * sides[1, s, h].astype(F32)
-                + 0.25 * (dot(wides[0, s], mp[h]) + rows_v[2 + h : 3 + h])
+        return [functools.partial(one, i) for i in range(chain_rows // chunk)]
+
+    def drop(s, chain):
+        at = rows_of(chain)
+
+        def one(h):
+            out = (
+                rows_v[h : h + 1] * sides[1, s, h, at].astype(F32)
+                + 0.25 * (dot(wides[0, s, at], mp[h]) + rows_v[2 + h : 3 + h])
             ).astype(BF16)
-            for h in range(2)
-        ]
-        for h, inner, outer in spans(s):
-            if s < SECTIONS - 1:
-                state[outer] = outs[h][inner]
-            else:
-                xs[outer] = outs[h][inner, :units]
-    net_start()
-    net_o[own] = xs[own]
-
-    def gather_grads(pairs, first=False, only=None):
-        turned = [[side[h].T[:units] for h in range(2)] for side, _ in pairs]
-        width = hidden_size // blocks
-        for b in range(blocks):
+            for side, inner, outer in spans(s, chain):
+                if side == h:
+                    start = inner.start - at.start
+                    state[outer] = out[start : start + inner.stop - inner.start]
+
+        return [functools.partial(one, h) for h in range(2)]
+
+    def lift_back(s, chain):
+        at = rows_of(chain)
+
+        def pairs():
+            for h, inner, outer in spans(s, chain):
+                sides[0, s, h, inner] = (0.25 * state[outer].astype(F32)).astype(BF16)
+
+        def add_up():
             for h in range(2):
-                term = sum(
-                    dot(turned[k][h], wide[:, b * width : (b + 1) * width])
-                    for k, (_, wide) in enumerate(pairs)
-                )
-                for c in range(width // LANES):
-                    at = b * block_rows + (2 * c + h) * units
-                    at = slice(at, at + units)
-                    block = term[:, c * LANES : (c + 1) * LANES]
-                    flat[at] = block if first else flat[at] + block
-            if only is not None:
-                only(b)
-
-    def mate_copies(s):
-        return [
-            remote(sides.at[1 - core, s], r_sides.at[s], mate_sem.at[0, s], mate),
-            remote(wides.at[1 - core, s], r_wides.at[s], mate_sem.at[1, s], mate),
-        ]
-
-    vec_mate = remote(v0, rvm, vm_sem, mate)
-    og_received()
-    state[:, :units] = gin[...]
-    for s in reversed(range(SECTIONS)):
-        grads = [None, None]
-        for h, inner, outer in spans(s):
-            sides[0, s, h, inner] = (0.25 * state[outer].astype(F32)).astype(BF16)
-        pre[...] = dot(sides[0, s, 0], mt[0]) + dot(sides[0, s, 1], mt[1])
-        for h in range(2):
-            value = 4.0 * sides[0, s, h].astype(F32)
-            gated = value * sides[1, s, h].astype(F32)
-            sums[h] += jnp.sum(value.reshape(-1, 8, value.shape[1]), 0)
-            sums[2 + h] += jnp.sum(gated.reshape(-1, 8, value.shape[1]), 0)
-        if s == 0:
-            for r in range(4):
-                v0[r : r + 1] = jnp.sum(sums[r], 0, keepdims=True)
-            vec_mate.start()
-
-        @pl.loop(0, half // chunk, unroll=4)
-        def _(i):
-            at = pl.ds(pl.multiple_of(i * chunk, chunk), chunk)
+                value = 4.0 * sides[0, s, h, at].astype(F32)
+                gated = value * sides[1, s, h, at].astype(F32)
+                sums[h] += jnp.sum(value.reshape(-1, 8, value.shape[1]), 0)
+                sums[2 + h] += jnp.sum(gated.reshape(-1, 8, value.shape[1]), 0)
+
+        return [pairs] + products(sides.at[0, s], mt, at) + [add_up]
+
+    def act_back(s, chain):
+        def one(i):
+            at = slice(chain * chain_rows + i * chunk, chain * chain_rows + (i + 1) * chunk)
             value = normed[s, at]
             grad = pre[at] * slope[s, at]
             grad = (
@@ -265,29 +283,103 @@
             ) * inv[s, at][:, :1]
             wides[1, s, at] = grad.astype(BF16)
 
+        return [functools.partial(one, i) for i in range(chain_rows // chunk)]
+
+    def drop_back(s, chain):
+        at = rows_of(chain)
+
+        def one(h):
+            back = dot(wides[1, s, at], wt[h])
+            for side, inner, outer in spans(s, chain):
+                if side == h:
+                    start = inner.start - at.start
+                    state[outer] = (
+                        rows_v[h : h + 1] * state[outer].astype(F32)
+                        + back[start : start + inner.stop - inner.start]
+                    ).astype(BF16)
+
+        return [functools.partial(one, h) for h in range(2)]
+
+    tok_received()
+    og_start()
+    split_chains(xin)
+    order = [(s, chain) for s in range(SECTIONS) for chain in range(chains)]
+    weave(lift(*order[0]))
+    for k, phase in enumerate(order):
+        beside = drop(*order[k - 1]) if k else []
+        if k + 1 < len(order):
+            beside += lift(*order[k + 1])
+        weave(act(*phase), beside)
+    weave(drop(*order[-1]))
+    join_chains(xs)
+    net_start()
+    net_o[own] = xs[own]
+
+    def gather_grads(pairs, first=False, only=None):
+        turned = {}
+
+        def turn(k, h):
+            turned[k, h] = pairs[k][0][h].T[:units]
+
+        def one(b, h):
+            term = sum(
+                dot(turned[k, h], wide[:, b * width : (b + 1) * width])
+                for k, (_, wide) in enumerate(pairs)
+            )
+            for c in range(width // LANES):
+                at = b * block_rows + (2 * c + h) * units
+                at = slice(at, at + units)
+                block = term[:, c * LANES : (c + 1) * LANES]
+                flat[at] = block if first else flat[at] + block
+            if only is not None and h == 1:
+                only(b)
+
+        steps = [functools.partial(turn, k, h) for k in range(len(pairs)) for h in range(2)]
+        return steps + [functools.partial(one, b, h) for b in range(blocks) for h in range(2)]
+
+    def mate_copies(s):
+        return [
+            remote(sides.at[1 - core, s], r_sides.at[s], mate_sem.at[0, s], mate),
+            remote(wides.at[1 - core, s], r_wides.at[s], mate_sem.at[1, s], mate),
+        ]
+
+    vec_mate = remote(v0, rvm, vm_sem, mate)
+    og_received()
+    split_chains(gin)
+
+    def own_pair(s):
+        return sides.at[core, s], wides.at[core, s]
+
+    def mate_pair(s):
         for copy in mate_copies(s):
-            copy.start()
-        for h in range(2):
-            back = dot(wides[1, s], wt[h])
-            grads[h] = back
-        for h, inner, outer in spans(s):
-            value = (
-                rows_v[h : h + 1] * (state[outer].astype(F32)) + grads[h][inner]
-            ).astype(BF16)
-            if s > 0:
-                state[outer] = value
-            else:
-                gs[outer] = value[:, :units]
-        if s == 0:
-            tg_start()
-            tg_o[own] = gs[own]
-        own_pair = (sides.at[core, s], wides.at[core, s])
-        if s == SECTIONS - 1:
-            gather_grads([own_pair], True)
+            copy.wait_recv()
+        return r_sides.at[s], r_wides.at[s]
+
+    order = [(s, chain) for s in reversed(range(SECTIONS)) for chain in range(chains)]
+    weave(lift_back(*order[0]))
+    for k, (s, chain) in enumerate(order):
+        beside = drop_back(*order[k - 1]) if k else []
+        if chain == 0 and s < SECTIONS - 1:
+            for copy in mate_copies(s + 1):
+                copy.start()
+            pairs = [own_pair(s + 1)]
+            if s < SECTIONS - 2:
+                pairs.append(mate_pair(s + 2))
+            beside += gather_grads(pairs, s == SECTIONS - 2)
+        if k + 1 < len(order):
+            beside += lift_back(*order[k + 1])
         else:
-            for copy in mate_copies(s + 1):
-                copy.wait_recv()
-            gather_grads([own_pair, (r_sides.at[s + 1], r_wides.at[s + 1])])
+            for r in range(4):
+                v0[r : r + 1] = jnp.sum(sums[r], 0, keepdims=True)
+            vec_mate.start()
+        weave(act_back(s, chain), beside)
+    for copy in mate_copies(0):
+        copy.start()
+    weave(drop_back(*order[-1]))
+    join_chains(gs)
+    tg_start()
+    tg_o[own] = gs[own]
+    weave(gather_grads([own_pair(0), mate_pair(1)]))
 
     def rows_at(b, first, size):
         return pl.ds(pl.multiple_of(b * block_rows + first, 16), size)
@@ -345,9 +437,7 @@
     v1[...] = v0[...] + rvm[...]
     for j in peers:
         vec_first(j).start()
-    for copy in mate_copies(0):
-        copy.wait_recv()
-    gather_grads([(r_sides.at[0], r_wides.at[0])], only=send_block)
+    weave(gather_grads([mate_pair(0)], only=send_block))
     for b in range(blocks):
         for j in peers:
             first_copy(b, j).wait_recv()

time: 62.5 us -> 60.8 us (0.973)
  Pallas kernels: 61.7 us -> 60 us
    pallas_call x1, Pallas kernels: 58.3 us -> 56.7 us  [on_device(): pl.pallas_call(functools.partial(step_kernel, n), out_shape=(jax.ShapeDty...]
where the time goes in v4:
time: 60.8 us; the launch traced here: 60.6 us
  Pallas kernels  60 us (99%)
  between operations  0.64 us (1%)
    pallas_call x1, Pallas kernels, on_device(): pl.pallas_call(functools.partial(step_kernel, n), out_shape=(jax.ShapeDty...  56.7 us
    pallas_call x1, Pallas kernels, on_device(): pl.pallas_call(functools.partial(finish_kernel, scale), out_shape=(jax.Sh...  3.34 us

profile of v4, /device:TPU:0, one launch (start us, length us, event | category | flops | bytes accessed | tf_op | source)
XLA Modules:
  0.0 60.6 jit_solution(5095617854133453746)
XLA Ops:
  0.6 56.7 %switch_step.1 = (bf16[512,192]{1,0:T(8,128)(2,1)}, bf16[512,192]{1,0:T(8,128)(2,1)}, bf16[2,2304,128]{2,1,0:T(8,128)(2,1)}, f32[4,256]{1,0:T(4,128)}) custom-call(bf16[192,512]{1,0:T(8,128)(2,1)} %bitcast.4, bf16[192,512]{1,0:T(8,128)(2,1)} %bitcast.5, bf16[384,768]{1,0:T(8,128)(2,1)} %sw.1, bf16[768,384]{1,0:T(8,128)(2,1)} %mw.1, f32[384]{0:T(512)} %bias.1, ...), custom_call_target="tpu_custom_call" | custom-call | tf_op jit(solution)/shard_map/switch_step/pallas_call | solution.py:559
  57.3 3.3 %finish.1 = (bf16[192,512]{1,0:T(8,128)(2,1)}, bf16[192,512]{1,0:T(8,128)(2,1)}, f32[384,768]{1,0:T(8,128)}, f32[768,384]{1,0:T(8,128)}, f32[384]{0:T(512)}, /*index=5*/f32[384]{0:T(512)}) custom-call(bf16[2,2304,128]{2,1,0:T(8,128)(2,1)} %get-tuple-element.16.res, bf16[512,192]{1,0:T(8,128)(2,1)} %get-tuple-element.17.net, ...), custom_call_target="tpu_custom_call" | custom-call | tf_op jit(solution)/shard_map/finish/pallas_call | solution.py:633

commit v5 on v4

--- a/solution.py
+++ b/solution.py
@@ -121,9 +121,6 @@
     loads[0].wait()
     tok_v[...] = xt[...].T
     xin[own] = tok_v[own]
-    loads[1].wait()
-    og_v[...] = gt[...].T
-    gin[own] = og_v[own]
     pl.semaphore_wait(barrier, GROUP + others - 1)
 
     def exchange(src, dst, number):
@@ -156,6 +153,9 @@
     net_start, net_received, net_sent = exchange(xs, net_o, 2)
     tg_start, tg_received, tg_sent = exchange(gs, tg_o, 3)
     tok_start()
+    loads[1].wait()
+    og_v[...] = gt[...].T
+    gin[own] = og_v[own]
 
     pad = wp.shape[1] - units
     loads[2].wait()
@@ -355,17 +355,26 @@
             copy.wait_recv()
         return r_sides.at[s], r_wides.at[s]
 
+    def send_wide(s, sender):
+        @pl.when(core == sender)
+        def _():
+            mate_copies(s)[1].start()
+
     order = [(s, chain) for s in reversed(range(SECTIONS)) for chain in range(chains)]
     weave(lift_back(*order[0]))
     for k, (s, chain) in enumerate(order):
         beside = drop_back(*order[k - 1]) if k else []
         if chain == 0 and s < SECTIONS - 1:
-            for copy in mate_copies(s + 1):
-                copy.start()
+            send_wide(s + 1, 0)
             pairs = [own_pair(s + 1)]
             if s < SECTIONS - 2:
                 pairs.append(mate_pair(s + 2))
             beside += gather_grads(pairs, s == SECTIONS - 2)
+        if chain == 1:
+            mate_copies(s)[0].start()
+            send_wide(s, 1)
+        if (s, chain) == (0, 1):
+            beside += gather_grads([mate_pair(1)])
         if k + 1 < len(order):
             beside += lift_back(*order[k + 1])
         else:
@@ -373,13 +382,7 @@
                 v0[r : r + 1] = jnp.sum(sums[r], 0, keepdims=True)
             vec_mate.start()
         weave(act_back(s, chain), beside)
-    for copy in mate_copies(0):
-        copy.start()
-    weave(drop_back(*order[-1]))
-    join_chains(gs)
-    tg_start()
-    tg_o[own] = gs[own]
-    weave(gather_grads([own_pair(0), mate_pair(1)]))
+    send_wide(0, 0)
 
     def rows_at(b, first, size):
         return pl.ds(pl.multiple_of(b * block_rows + first, 16), size)
@@ -433,11 +436,19 @@
         for j in peers:
             first_copy(b, j).start()
 
+    def last_terms():
+        weave(gather_grads([own_pair(0), mate_pair(0)], only=send_block))
+
+    pl.when(core == 0)(last_terms)
+    weave(drop_back(*order[-1]))
+    join_chains(gs)
+    tg_start()
+    tg_o[own] = gs[own]
+    pl.when(core == 1)(last_terms)
     vec_mate.wait_recv()
     v1[...] = v0[...] + rvm[...]
     for j in peers:
         vec_first(j).start()
-    weave(gather_grads([mate_pair(0)], only=send_block))
     for b in range(blocks):
         for j in peers:
             first_copy(b, j).wait_recv()
@@ -517,19 +528,35 @@
             mate_copy(b, j).wait()
 
 
-def finish_kernel(scale, res, net, tg, vec, gate, net_o, tg_o, spread_o, merge_o, bias_o, gate_o):
+def finish_kernel(
+    scale, res, net, tg, vec, gate, net_o, tg_o, spread_out, merge_out, bias_o, gate_o,
+    spread_o, merge_o, sems,
+):
     units = net.shape[1]
     tall, wide = spread_o.shape
-    net_o[...] = net[...].T
-    tg_o[...] = tg[...].T
+    copies = []
     for c in range(wide // LANES):
         across = slice(c * LANES, (c + 1) * LANES)
         spread_o[:, across] = res[1, c * tall : (c + 1) * tall].astype(F32) * scale
+        copies.append(
+            pltpu.make_async_copy(
+                spread_o.at[:, across], spread_out.at[:, across], sems.at[0, c]
+            )
+        )
+        copies[-1].start()
+    for c in range(wide // LANES):
+        across = slice(c * LANES, (c + 1) * LANES)
         for k in range(tall // LANES):
             at = c * tall + k * LANES
             merge_o[across, k * LANES : (k + 1) * LANES] = (
                 res[0, at : at + LANES].astype(F32) * scale
             ).T
+        copies.append(
+            pltpu.make_async_copy(merge_o.at[across], merge_out.at[across], sems.at[1, c])
+        )
+        copies[-1].start()
+    net_o[...] = net[...].T
+    tg_o[...] = tg[...].T
     opened = jax.nn.sigmoid(gate[...])
     opened = opened * (1.0 - opened) * scale
     both = [
@@ -537,6 +564,8 @@
     ]
     bias_o[...] = both[0].reshape(-1) * (0.25 * scale)
     gate_o[...] = both[1].reshape(-1) * opened
+    for copy in copies:
+        copy.wait()
 
 
 def on_device(tokens, out_grad, spread_weight, merge_weight, switch_bias, gate_logit):
@@ -641,7 +670,12 @@
             jax.ShapeDtypeStruct((switch,), F32),
         ),
         in_specs=[vmem_spec] * 5,
-        out_specs=(vmem_spec,) * 6,
+        out_specs=(vmem_spec, vmem_spec, any_spec, any_spec, vmem_spec, vmem_spec),
+        scratch_shapes=[
+            vmem((switch, hidden_size), F32),
+            vmem((hidden_size, switch), F32),
+            dma((2, hidden_size // LANES)),
+        ],
         compiler_params=pltpu.CompilerParams(vmem_limit_bytes=61 * 2**20),
         name="finish",
     )(res, net, tg, vec, gate_logit)

time: 60.8 us -> 63 us (1.036)
  Pallas kernels: 60 us -> 62.2 us
    pallas_call x1, Pallas kernels: 56.7 us -> 58.5 us  [on_device(): pl.pallas_call(functools.partial(step_kernel, n), out_shape=(jax.ShapeDty...]
where the time goes in v5:
time: 63 us; the launch traced here: 62.9 us
  Pallas kernels  62.2 us (99%)
  between operations  0.64 us (1%)
    pallas_call x1, Pallas kernels, on_device(): pl.pallas_call(functools.partial(step_kernel, n), out_shape=(jax.ShapeDty...  58.5 us
    pallas_call x1, Pallas kernels, on_device(): pl.pallas_call(functools.partial(finish_kernel, scale), out_shape=(jax.Sh...  3.72 us

profile of v5, /device:TPU:0, one launch (start us, length us, event | category | flops | bytes accessed | tf_op | source)
XLA Modules:
  0.0 62.9 jit_solution(17708119799457280424)
XLA Ops:
  0.6 58.5 %switch_step.1 = (bf16[512,192]{1,0:T(8,128)(2,1)}, bf16[512,192]{1,0:T(8,128)(2,1)}, bf16[2,2304,128]{2,1,0:T(8,128)(2,1)}, f32[4,256]{1,0:T(4,128)}) custom-call(bf16[192,512]{1,0:T(8,128)(2,1)} %bitcast.4, bf16[192,512]{1,0:T(8,128)(2,1)} %bitcast.5, bf16[384,768]{1,0:T(8,128)(2,1)} %sw.1, bf16[768,384]{1,0:T(8,128)(2,1)} %mw.1, f32[384]{0:T(512)} %bias.1, ...), custom_call_target="tpu_custom_call" | custom-call | tf_op jit(solution)/shard_map/switch_step/pallas_call | solution.py:588
  59.1 3.7 %finish.1 = (bf16[192,512]{1,0:T(8,128)(2,1)}, bf16[192,512]{1,0:T(8,128)(2,1)}, f32[384,768]{1,0:T(8,128)}, f32[768,384]{1,0:T(8,128)}, f32[384]{0:T(512)}, /*index=5*/f32[384]{0:T(512)}) custom-call(bf16[2,2304,128]{2,1,0:T(8,128)(2,1)} %get-tuple-element.16.res, bf16[512,192]{1,0:T(8,128)(2,1)} %get-tuple-element.17.net, ...), custom_call_target="tpu_custom_call" | custom-call | tf_op jit(solution)/shard_map/finish/pallas_call | solution.py:662

commit v6 on v4

--- a/solution.py
+++ b/solution.py
@@ -121,9 +121,6 @@
     loads[0].wait()
     tok_v[...] = xt[...].T
     xin[own] = tok_v[own]
-    loads[1].wait()
-    og_v[...] = gt[...].T
-    gin[own] = og_v[own]
     pl.semaphore_wait(barrier, GROUP + others - 1)
 
     def exchange(src, dst, number):
@@ -156,6 +153,9 @@
     net_start, net_received, net_sent = exchange(xs, net_o, 2)
     tg_start, tg_received, tg_sent = exchange(gs, tg_o, 3)
     tok_start()
+    loads[1].wait()
+    og_v[...] = gt[...].T
+    gin[own] = og_v[own]
 
     pad = wp.shape[1] - units
     loads[2].wait()
@@ -330,7 +330,10 @@
                 at = b * block_rows + (2 * c + h) * units
                 at = slice(at, at + units)
                 block = term[:, c * LANES : (c + 1) * LANES]
-                flat[at] = block if first else flat[at] + block
+                block = block if first else flat[at] + block
+                flat[at] = block
+                if only is not None:
+                    flat_b[at] = block.astype(BF16)
             if only is not None and h == 1:
                 only(b)
 
@@ -355,17 +358,26 @@
             copy.wait_recv()
         return r_sides.at[s], r_wides.at[s]
 
+    def send_wide(s, sender):
+        @pl.when(core == sender)
+        def _():
+            mate_copies(s)[1].start()
+
     order = [(s, chain) for s in reversed(range(SECTIONS)) for chain in range(chains)]
     weave(lift_back(*order[0]))
     for k, (s, chain) in enumerate(order):
         beside = drop_back(*order[k - 1]) if k else []
         if chain == 0 and s < SECTIONS - 1:
-            for copy in mate_copies(s + 1):
-                copy.start()
+            send_wide(s + 1, 0)
             pairs = [own_pair(s + 1)]
             if s < SECTIONS - 2:
                 pairs.append(mate_pair(s + 2))
             beside += gather_grads(pairs, s == SECTIONS - 2)
+        if chain == 1:
+            mate_copies(s)[0].start()
+            send_wide(s, 1)
+        if (s, chain) == (0, 1):
+            beside += gather_grads([mate_pair(1)])
         if k + 1 < len(order):
             beside += lift_back(*order[k + 1])
         else:
@@ -373,13 +385,11 @@
                 v0[r : r + 1] = jnp.sum(sums[r], 0, keepdims=True)
             vec_mate.start()
         weave(act_back(s, chain), beside)
-    for copy in mate_copies(0):
-        copy.start()
-    weave(drop_back(*order[-1]))
+    send_wide(0, 0)
+    weave(drop_back(*order[-1]), gather_grads([own_pair(0)]))
     join_chains(gs)
     tg_start()
     tg_o[own] = gs[own]
-    weave(gather_grads([own_pair(0), mate_pair(1)]))
 
     def rows_at(b, first, size):
         return pl.ds(pl.multiple_of(b * block_rows + first, 16), size)
@@ -428,8 +438,6 @@
     peers = range(1, SIDE)
 
     def send_block(b):
-        at = slice(b * block_rows, (b + 1) * block_rows)
-        flat_b[at] = flat[at].astype(BF16)
         for j in peers:
             first_copy(b, j).start()
 
@@ -437,7 +445,11 @@
     v1[...] = v0[...] + rvm[...]
     for j in peers:
         vec_first(j).start()
-    weave(gather_grads([mate_pair(0)], only=send_block))
+    mate_copies(0)[0].wait_recv()
+    final = gather_grads([(r_sides.at[0], r_wides.at[0])], only=send_block)
+    weave(final[:2])
+    mate_copies(0)[1].wait_recv()
+    weave(final[2:])
     for b in range(blocks):
         for j in peers:
             first_copy(b, j).wait_recv()

time: 60.8 us -> 61.6 us (1.013)
  Pallas kernels: 60 us -> 60.8 us
    pallas_call x1, Pallas kernels: 56.7 us -> 57.4 us  [on_device(): pl.pallas_call(functools.partial(step_kernel, n), out_shape=(jax.ShapeDty...]
where the time goes in v6:
time: 61.6 us; the launch traced here: 61.4 us
  Pallas kernels  60.8 us (99%)
  between operations  0.64 us (1%)
    pallas_call x1, Pallas kernels, on_device(): pl.pallas_call(functools.partial(step_kernel, n), out_shape=(jax.ShapeDty...  57.4 us
    pallas_call x1, Pallas kernels, on_device(): pl.pallas_call(functools.partial(finish_kernel, scale), out_shape=(jax.Sh...  3.34 us

profile of v6, /device:TPU:0, one launch (start us, length us, event | category | flops | bytes accessed | tf_op | source)
XLA Modules:
  0.0 61.4 jit_solution(17496174862353888433)
XLA Ops:
  0.6 57.4 %switch_step.1 = (bf16[512,192]{1,0:T(8,128)(2,1)}, bf16[512,192]{1,0:T(8,128)(2,1)}, bf16[2,2304,128]{2,1,0:T(8,128)(2,1)}, f32[4,256]{1,0:T(4,128)}) custom-call(bf16[192,512]{1,0:T(8,128)(2,1)} %bitcast.4, bf16[192,512]{1,0:T(8,128)(2,1)} %bitcast.5, bf16[384,768]{1,0:T(8,128)(2,1)} %sw.1, bf16[768,384]{1,0:T(8,128)(2,1)} %mw.1, f32[384]{0:T(512)} %bias.1, ...), custom_call_target="tpu_custom_call" | custom-call | tf_op jit(solution)/shard_map/switch_step/pallas_call | solution.py:571
  58.1 3.3 %finish.1 = (bf16[192,512]{1,0:T(8,128)(2,1)}, bf16[192,512]{1,0:T(8,128)(2,1)}, f32[384,768]{1,0:T(8,128)}, f32[768,384]{1,0:T(8,128)}, f32[384]{0:T(512)}, /*index=5*/f32[384]{0:T(512)}) custom-call(bf16[2,2304,128]{2,1,0:T(8,128)(2,1)} %get-tuple-element.16.res, bf16[512,192]{1,0:T(8,128)(2,1)} %get-tuple-element.17.net, ...), custom_call_target="tpu_custom_call" | custom-call | tf_op jit(solution)/shard_map/finish/pallas_call | solution.py:645
